TPU v7x, 32 devices: a whole 2x2x4 slice. The times are simulated.
32 devices in a mesh: af: 4 (over y, x), sa: 8 (over z, core).
Axes of the slice: x: 2, y: 2, z: 4, core: 2. Of those that a mesh axis runs over, the one named last changes fastest.
Arguments:
- pressure: bfloat16 [4, 32, 1024, 2048], P(None, 'af', 'sa'), may hold values from -6 to 6
- legendre: bfloat16 [512, 1025, 512], P(('af', 'sa')), may hold values from -0.1875 to 0.1875
- radial: bfloat16 [1024, 32, 128], replicated, may hold values from -1 to 1
Outputs:
- shells: bfloat16 [512, 1025, 2, 4, 128], P(('af', 'sa'))
All inputs are finite; a program needn't handle non-finite values.
Results may differ from a plain program's by a relative error of at most 0.0071.
Values may be sent and summed in bfloat16 or wider, within the bound.
No kernel may reach another device: no remote copies, remote signals or barrier semaphores. Data moves between devices by JAX's collectives and lax.ppermute only.
A program may use at most 448 MiB of HBM per device.

v0:
```python
import math

import jax
import jax.numpy as jnp
from jax import lax
from jax.sharding import PartitionSpec as P

LDEG = 1024


def order_of_column(column_count):
    column = lax.iota(jnp.int32, column_count)
    halves = column // 2
    return jnp.where(column % 2 == 0, halves, LDEG - 1 - halves)


def fourier_table(lon_count, orders):
    longitude = lax.iota(jnp.int32, lon_count)
    product = longitude[:, None] * orders[None, :] % lon_count
    phases = product.astype(jnp.float32) * (2.0 * math.pi / lon_count)
    norm_scale = 1.0 / math.sqrt(lon_count)
    return jnp.stack([jnp.cos(phases) * norm_scale, -jnp.sin(phases) * norm_scale], axis=1).astype(
        jnp.bfloat16
    )


def pair_layout(pair_index):
    column = lax.iota(jnp.int32, LDEG + 1)
    segment = (column >= LDEG - pair_index).astype(jnp.int32)
    order_here = jnp.where(segment == 1, LDEG - 1 - pair_index, pair_index)
    degree = jnp.where(segment == 1, column - 1, pair_index + column)
    parity = (degree + order_here) % 2
    return (segment, degree, parity)


def selector(segment, parity):
    branch_ids = lax.iota(jnp.int32, 2)
    seg_match = segment[..., None, None, :] == branch_ids[:, None, None]
    par_match = parity[..., None, None, :] == branch_ids[None, :, None]
    return (seg_match & par_match).astype(jnp.float32)


def harmonics(gathered, legendre, select):
    parts, per_device, frame_count, freqs, lat_count = gathered.shape
    half_count = lat_count // 2
    upper_half = gathered[..., :half_count].astype(jnp.float32)
    lower_half = jnp.flip(gathered[..., half_count:], axis=4).astype(jnp.float32)
    even_part = (upper_half + lower_half).astype(jnp.bfloat16)
    odd_part = (upper_half - lower_half).astype(jnp.bfloat16)
    folded = jnp.stack([even_part, odd_part], axis=2)
    folded = folded.reshape(parts, per_device // 2, 2, 2, frame_count, freqs, half_count)
    products = jnp.einsum(
        "rkstxfj,kqj->krstxfq", folded, legendre, preferred_element_type=jnp.float32
    )
    return jnp.sum(products * select[:, None, :, :, None, None, :], axis=(2, 3)).astype(
        jnp.bfloat16
    )


def on_device(pressure, legendre, radial):
    frames, freq_dev, lat_dev, lon_count = pressure.shape
    af_count = lax.axis_size("af")
    sa_count = lax.axis_size("sa")
    per_device = LDEG // (af_count * sa_count)
    trig_table = fourier_table(lon_count, order_of_column(LDEG))
    spectra = jnp.einsum(
        "krc,xfjk->rcxfj", trig_table, pressure, preferred_element_type=jnp.float32
    ).astype(jnp.bfloat16)
    pairs_here = legendre.shape[0]
    owner_block = lax.axis_index("af") * sa_count + lax.axis_index("sa")
    pair_ids = owner_block * pairs_here + lax.iota(jnp.int32, pairs_here)
    segment, degree, parity = pair_layout(pair_ids[:, None])
    select = selector(segment, parity)
    spread = spectra.reshape(1, 2, af_count * sa_count, per_device, frames, freq_dev, lat_dev)
    piece = lax.all_to_all(spread, ("af", "sa"), split_axis=2, concat_axis=0, tiled=True)
    frame_count = piece.shape[4]
    sources = piece.reshape(af_count, sa_count, 2, per_device, frame_count, freq_dev, lat_dev)
    sources = jnp.transpose(sources, (2, 3, 4, 0, 5, 1, 6))
    gathered = sources.reshape(2, per_device, frame_count, af_count * freq_dev, sa_count * lat_dev)
    harmonic = harmonics(gathered, legendre, select)
    factors = jnp.take(radial, degree.reshape(-1), axis=0)
    factors = factors.reshape(pairs_here, LDEG + 1, radial.shape[1], radial.shape[2])
    result = jnp.einsum("krxfq,kqfs->kqrxs", harmonic, factors, preferred_element_type=jnp.float32)
    return result.astype(jnp.bfloat16)


def solution(mesh):
    return jax.shard_map(
        on_device,
        mesh=mesh,
        in_specs=(P(None, "af", "sa", None), P(("af", "sa"), None, None), P()),
        out_specs=P(("af", "sa"), None, None, None, None),
        check_vma=False,
    )
```

profile of v0, /device:TPU:0, one launch (start us, length us, event | category | flops | bytes accessed | tf_op | source)
XLA Modules:
  0.0 828.0 jit_solution(938541630663302989)
XLA Ops:
  0.0 37.2 %multiply_convert_fusion.1 = (bf16[2048,1,1024]{0,2,1:T(8,128)(2,1)}, bf16[2048,1,1024]{0,2,1:T(8,128)(2,1)}) fusion(s32[1024]{0:T(1024)S(1)} %subtract_select_fusion), kind=kLoop, calls=%fused_computation.28 | loop fusion | flops 39845888 | bytes 8392704 | tf_op jit(solution)/shard_map/convert
  37.2 39.9 %fusion.14 = bf16[2,1024,4,8,128]{4,1,3,2,0:T(8,128)(2,1)S(1)} fusion(bf16[4,8,128,2048]{3,2,1,0:T(8,128)(2,1)} %param.3, bf16[2048,1,1024]{0,2,1:T(8,128)(2,1)} %get-tuple-element.10, bf16[2048,1,1024]{0,2,1:T(8,128)(2,1)} %get-tuple-element.9), kind=kOutput, calls=%fused_computation.17 | convolution fusion | flops 34384904192 | bytes 41943040 | tf_op jit(solution)/shard_map/krc,xfjk->rcxfj/dot_general | solution.py:66
  77.0 11.7 %copy.12 = bf16[1,2,32,32,4,8,128]{6,5,4,3,1,0,2:T(8,128)(2,1)} copy(bf16[1,2,32,32,4,8,128]{6,3,2,5,4,1,0:T(8,128)(2,1)S(1)} %bitcast.38) | data formatting | bytes 33554432 | tf_op jit(solution)/shard_map/reshape | solution.py:74
  88.8 7.6 all-to-all-start
  96.4 0.1 add_select_fusion.2
  96.5 0.2 select_n.122
  96.7 0.2 fusion.27
  96.9 56.7 %gather_fusion = bf16[16400,32,128]{2,1,0:T(8,128)(2,1)} fusion(bf16[1024,32,128]{2,1,0:T(8,128)(2,1)} %param.5, s32[17408]{0:T(1024)S(1)} %pad_clamp_fusion), kind=kCustom, calls=%fused_computation | custom fusion | bytes 268763200 | tf_op jit(solution)/shard_map/jit(_take)/gather | solution.py:81
  153.6 0.1 compare_and_fusion
  153.7 0.1 iota_compare_fusion.1
  153.8 0.1 iota_compare_fusion
  153.9 0.2 and_convert_fusion
  154.1 306.8 %all-to-all-done = bf16[1,2,32,32,4,8,128]{6,5,4,3,1,0,2:T(8,128)(2,1)} async-done(((bf16[1,2,32,32,4,8,128]{6,5,4,3,1,0,2:T(8,128)(2,1)}), bf16[1,2,32,32,4,8,128]{6,5,4,3,1,0,2:T(8,128)(2,1)}, u32[]{:S(2)}, u32[]{:S(2)}) %all-to-all-start) | async-done | bytes 16777248 | tf_op jit(solution)/shard_map/all_to_all | solution.py:75
  460.9 32.2 %copy.13 = bf16[2,32,4,4,8,8,128]{6,5,4,3,2,1,0:T(8,128)(2,1)} copy(bf16[2,32,4,4,8,8,128]{6,4,2,1,0,5,3:T(8,128)(2,1)} %bitcast.7) | data formatting | bytes 33554432 | tf_op jit(solution)/shard_map/transpose | solution.py:78
  493.1 25.3 %reshape.354 = bf16[2,32,4,32,1024]{4,3,2,1,0:T(8,128)(2,1)} reshape(bf16[2,32,4,4,8,8,128]{6,5,4,3,2,1,0:T(8,128)(2,1)} %copy.13) | data formatting | bytes 33554432 | tf_op jit(solution)/shard_map/reshape | solution.py:79
  518.4 8.5 %slice.11 = bf16[2,32,4,32,512]{4,3,2,1,0:T(8,128)(2,1)} slice(bf16[2,32,4,32,1024]{4,3,2,1,0:T(8,128)(2,1)} %reshape.354), slice={[0:2], [0:32], [0:4], [0:32], [512:1024]} | slice | bytes 16777216 | tf_op jit(solution)/shard_map/slice | solution.py:47
  526.8 21.1 %rev.4 = bf16[2,32,4,32,512]{4,3,2,1,0:T(8,128)(2,1)} reverse(bf16[2,32,4,32,512]{4,3,2,1,0:T(8,128)(2,1)} %slice.11), dimensions={4} | reverse | bytes 16777216 | tf_op jit(solution)/shard_map/jit(_flip)/rev | solution.py:47
  547.9 13.6 %fusion.9 = (bf16[2,32,4,32,512]{4,3,2,1,0:T(8,128)(2,1)}, bf16[2,32,4,32,512]{4,3,2,1,0:T(8,128)(2,1)}) fusion(bf16[2,32,4,32,512]{4,3,2,1,0:T(8,128)(2,1)} %rev.4, bf16[2,32,4,32,1024]{4,3,2,1,0:T(8,128)(2,1)} %reshape.354), kind=kLoop, calls=%fused_computation.11 | loop fusion | flops 25165824 | bytes 33554432 | tf_op jit(solution)/shard_map/convert_element_type | solution.py:48
  561.5 148.2 %multiply_reduce_fusion = bf16[16,2,4,32,1025]{4,3,2,1,0:T(8,128)(2,1)} fusion(f32[16,2,2,1025]{3,2,1,0:T(2,128)S(1)} %and_convert_fusion, bf16[16,1025,512,1,1,1,1]{2,0,1,6,5,4,3:T(8,128)(2,1)} %bitcast.41, bf16[2,16,2,1,4,32,512]{6,5,4,2,1,0,3:T(8,128)(2,1)} %bitcast.40, bf16[2,16,2,1,4,32,512]{6,5,4,2,1,0,3:T(8,128)(2,1)} %bitcast.39), kind=kOutput, calls=%fused_computation.5 | convolution fusion | flops 17234423808 | bytes 42230016 | tf_op jit(solution)/shard_map/rkstxfj,kqj->krstxfq/dot_general | solution.py:52
  709.8 46.9 %copy.17 = bf16[16,2,4,32,1025]{3,2,1,4,0:T(4,128)(2,1)} copy(bf16[16,2,4,32,1025]{4,3,2,1,0:T(8,128)(2,1)} %multiply_reduce_fusion) | data formatting | bytes 16793600 | tf_op jit(solution)/shard_map/convert_element_type | solution.py:55
  756.6 71.3 %fusion.5 = bf16[16,1025,2,4,128]{4,3,2,1,0:T(4,128)(2,1)} fusion(bf16[16,2,4,32,1025]{3,2,1,4,0:T(4,128)(2,1)} %copy.17, bf16[16,1025,32,128]{3,2,1,0:T(8,128)(2,1)} %bitcast.11, pred[16,1025]{1,0:T(8,128)(4,1)S(1)} %get-tuple-element.11), kind=kOutput, calls=%fused_computation.7 | convolution fusion | flops 1158758400 | bytes 176349200 | tf_op jit(solution)/shard_map/krxfq,kqfs->kqrxs/dot_general | solution.py:83
  (5 shorter events, 0.0 us)
Async XLA Ops:
  88.8 372.1 %all-to-all-start = ((bf16[1,2,32,32,4,8,128]{6,5,4,3,1,0,2:T(8,128)(2,1)}), bf16[1,2,32,32,4,8,128]{6,5,4,3,1,0,2:T(8,128)(2,1)}, u32[]{:S(2)}, u32[]{:S(2)}) async-start(bf16[1,2,32,32,4,8,128]{6,5,4,3,1,0,2:T(8,128)(2,1)} %copy.12), calls=%async_computation | async-start | bytes 33554432 | tf_op jit(solution)/shard_map/all_to_all | solution.py:75
where the time goes:
time: 831 us; the launch traced here: 828 us
  waiting for transfers between devices  307 us (37%)
  matrix products  259 us (31%)
  local copies, waits for them, and re-layouts  203 us (24%)
  other arithmetic  51.6 us (6%)
    all_to_all x1, waiting for transfers between devices, on_device(): lax.all_to_all(spread, ('af', 'sa'), split_axis=2, concat_axis=0, tiled=T...  307 us
    dot_general x1, matrix products, harmonics(): jnp.einsum('rkstxfj,kqj->krstxfq', folded, legendre, preferred_element_ty...  148 us
    dot_general x1, matrix products, on_device(): jnp.einsum('krxfq,kqfs->kqrxs', harmonic, factors, preferred_element_type...  71.3 us
    gather x1, local copies, waits for them, and re-layouts, on_device(): factors = jnp.take(radial, degree.reshape(-1), axis=0)  56.7 us
    convert_element_type x1, local copies, waits for them, and re-layouts, harmonics(): jnp.sum(products * select[:, None, :, :, None, None, :], axis=(2, 3))  46.9 us
    dot_general x1, matrix products, on_device(): jnp.einsum('krc,xfjk->rcxfj', trig_table, pressure, preferred_element_typ...  39.9 us
    another operation x1, other arithmetic  37.2 us
    transpose x1, local copies, waits for them, and re-layouts, on_device(): sources = jnp.transpose(sources, (2, 3, 4, 0, 5, 1, 6))  32.2 us
  transfers between devices with their start and end apart: 1, of which 1 were waited for; matrix products, arithmetic and copies ran while one was open for 7% of the time, Pallas kernels for 0%

commit v1 on v0

--- a/solution.py
+++ b/solution.py
@@ -2,10 +2,15 @@
 
 import jax
 import jax.numpy as jnp
+import numpy as np
 from jax import lax
+from jax.experimental import pallas as pl
+from jax.experimental.pallas import tpu as pltpu
 from jax.sharding import PartitionSpec as P
 
 LDEG = 1024
+CHUNKS = (2, 5, 5, 3, 1)
+VMEM_LIMIT = 62 * 1024 * 1024
 
 
 def order_of_column(column_count):
@@ -57,7 +62,7 @@
     )
 
 
-def on_device(pressure, legendre, radial):
+def plain_on_device(pressure, legendre, radial):
     frames, freq_dev, lat_dev, lon_count = pressure.shape
     af_count = lax.axis_size("af")
     sa_count = lax.axis_size("sa")
@@ -84,6 +89,216 @@
     return result.astype(jnp.bfloat16)
 
 
+def table_rows(lon_count, devices, pairs_here, first, count):
+    pair = np.arange(devices)[:, None] * pairs_here + first + np.arange(count)[None, :]
+    order = np.stack([pair, LDEG - 1 - pair], axis=1)
+    product = (order[..., None].astype(np.int64) * np.arange(lon_count)) % lon_count
+    phase = product.astype(np.float32) * np.float32(2.0 * math.pi / lon_count)
+    scale = np.float32(1.0 / math.sqrt(lon_count))
+    rows = np.stack([np.cos(phase) * scale, -np.sin(phase) * scale], axis=1)
+    return rows.reshape(devices * 4 * count, lon_count).astype(jnp.bfloat16)
+
+
+def dot_t(a, b):
+    return lax.dot_general(a, b, (((1,), (1,)), ((), ())), preferred_element_type=jnp.float32)
+
+
+def dft_kernel(table_ref, pressure_ref, out_ref, acc_ref):
+    rows = table_ref.shape[0]
+    frame = pl.program_id(0)
+    for f in range(0, 8, 2):
+        block = pressure_ref[0, f : f + 2].reshape(256, pressure_ref.shape[3])
+        both = dot_t(table_ref[...], block)
+        at = (frame % 2) * 8 + f
+        acc_ref[pl.ds(at, rows, stride=16), :] = both[:, :128]
+        acc_ref[pl.ds(at + 1, rows, stride=16), :] = both[:, 128:]
+
+    @pl.when(frame % 2 == 1)
+    def _():
+        out_ref[...] = acc_ref[...].reshape(rows, 16, 128).astype(jnp.bfloat16)
+
+
+def dft(table, pressure):
+    rows, lon_count = table.shape
+    return pl.pallas_call(
+        dft_kernel,
+        grid=(4,),
+        in_specs=[
+            pl.BlockSpec((rows, lon_count), lambda x: (0, 0), pipeline_mode=pl.Buffered(1)),
+            pl.BlockSpec((1, 8, 128, lon_count), lambda x: (x, 0, 0, 0)),
+        ],
+        out_specs=pl.BlockSpec((rows, 16, 128), lambda x: (0, x // 2, 0)),
+        out_shape=jax.ShapeDtypeStruct((rows, 32, 128), jnp.bfloat16),
+        scratch_shapes=[pltpu.VMEM((rows * 16, 128), jnp.float32)],
+        compiler_params=pltpu.CompilerParams(vmem_limit_bytes=VMEM_LIMIT),
+        cost_estimate=pl.CostEstimate(
+            flops=2 * rows * 4096 * lon_count, bytes_accessed=1 << 24, transcendentals=0
+        ),
+        name="dft_piece",
+    )(table, pressure)
+
+
+def shells_kernel(first, *refs):
+    base_ref, recv_ref, leg_ref, rad_ref, pick_ref, flip_ref = refs[:6]
+    out_ref, both_ref, harm_ref, copies_ref, result_ref = refs[-5:]
+    pair = base_ref[0] + first + pl.program_id(0)
+    bound = LDEG - pair
+
+    for s in range(4):
+        lanes = slice(128 * s, 128 * s + 128)
+        for seg in range(2):
+            mirrored = []
+            for r in range(2):
+                for a in range(4):
+                    row = 128 * r + 32 * a
+                    both_ref[seg, row : row + 32, lanes] = recv_ref[8 * a + s, r, seg, 0]
+                    mirrored.append(recv_ref[8 * a + 7 - s, r, seg, 0])
+            mirrored = jnp.concatenate(mirrored, axis=0)
+            turned = jnp.dot(mirrored, flip_ref[...], preferred_element_type=jnp.float32)
+            both_ref[seg, 256:512, lanes] = turned.astype(jnp.bfloat16)
+
+    own_q = (
+        lax.broadcasted_iota(jnp.int32, (64, 256), 1) // 32
+        == lax.broadcasted_iota(jnp.int32, (64, 256), 0) % 8
+    )
+
+    def legendre_rows(rows, start, seg):
+        product = dot_t(rows, both_ref[seg])
+        q = start + lax.broadcasted_iota(jnp.int32, (rows.shape[0], 256), 0)
+        parity = (q + seg * pair) % 2
+        north, south = product[:, :256], product[:, 256:]
+        return q, north + jnp.where(parity == 0, south, -south)
+
+    def degree(q):
+        return jnp.where(q >= bound, q - 1, pair + q)
+
+    def factors_at(degree_here):
+        return rad_ref[pl.ds(pl.multiple_of(degree_here * 32, 32), 32), :]
+
+    def fill_copies(harm):
+        harm = harm.astype(jnp.bfloat16)
+        for rx in range(8):
+            copies_ref[rx, 0 : harm.shape[0]] = jnp.dot(
+                harm, pick_ref[rx], preferred_element_type=jnp.float32
+            )
+
+    def radial_block(block, slab):
+        rows = [copies_ref[rx, 8 * block : 8 * block + 8] for rx in range(8)]
+        diagonal = jnp.where(own_q, jnp.concatenate(rows, axis=0), 0.0).astype(jnp.bfloat16)
+        result = jnp.dot(diagonal, slab, preferred_element_type=jnp.float32)
+        for rx in range(8):
+            result_ref[pl.ds(64 * block + rx, 8, stride=8), :] = result[8 * rx : 8 * rx + 8]
+
+    @pl.loop(0, 8)
+    def _(tile):
+        start = pl.multiple_of(tile * 128, 128)
+        rows = leg_ref[0, pl.ds(start, 128), :]
+
+        @pl.when(start < bound)
+        def _():
+            _, harm = legendre_rows(rows, start, 0)
+            harm_ref[...] = harm
+
+        @pl.when(start + 128 > bound)
+        def _():
+            q, harm = legendre_rows(rows, start, 1)
+            harm_ref[...] = jnp.where(q >= bound, harm, harm_ref[...])
+
+        fill_copies(harm_ref[...])
+        for block in range(16):
+            slab = [factors_at(degree(start + 8 * block + k)) for k in range(8)]
+            radial_block(block, jnp.concatenate(slab, axis=0))
+        at = pl.multiple_of(start * 8, 1024)
+        out_ref[0, pl.ds(at, 1024), :] = result_ref[...].astype(jnp.bfloat16)
+
+    rows = jnp.broadcast_to(leg_ref[0, LDEG : LDEG + 1, :].astype(jnp.float32), (16, 512))
+    _, harm = legendre_rows(rows.astype(jnp.bfloat16), LDEG, 1)
+    fill_copies(jnp.broadcast_to(harm[0:1], (16, 256)))
+    radial_block(0, jnp.concatenate([factors_at(LDEG - 1)] * 8, axis=0))
+    out_ref[0, 8 * LDEG : 8 * LDEG + 8, :] = result_ref[0:8].astype(jnp.bfloat16)
+
+
+def shells_piece(base, received, legendre, radial, pick, flip, output, first, count):
+    pairs_here = legendre.shape[0]
+    rows = 8 * (LDEG + 1)
+    once = pl.Buffered(1)
+    in_specs = [
+        pl.BlockSpec(memory_space=pltpu.SMEM),
+        pl.BlockSpec((32, 2, 2, 1, 32, 128), lambda i: (0, 0, 0, i, 0, 0)),
+        pl.BlockSpec((1, LDEG + 1, 512), lambda i: (first + i, 0, 0)),
+        pl.BlockSpec(radial.shape, lambda i: (0, 0), pipeline_mode=once),
+        pl.BlockSpec((8, 256, 256), lambda i: (0, 0, 0)),
+        pl.BlockSpec((128, 128), lambda i: (0, 0)),
+    ]
+    operands = [base, received, legendre, radial, pick, flip]
+    aliases = {}
+    if output is not None:
+        in_specs.append(pl.BlockSpec(memory_space=pl.ANY))
+        operands.append(output)
+        aliases = {6: 0}
+
+    def kernel(*refs):
+        shells_kernel(first, *refs)
+
+    return pl.pallas_call(
+        kernel,
+        grid=(count,),
+        in_specs=in_specs,
+        out_specs=pl.BlockSpec((1, rows, 128), lambda i: (first + i, 0, 0)),
+        out_shape=jax.ShapeDtypeStruct((pairs_here, rows, 128), jnp.bfloat16),
+        scratch_shapes=[
+            pltpu.VMEM((2, 512, 512), jnp.bfloat16),
+            pltpu.VMEM((128, 256), jnp.float32),
+            pltpu.VMEM((8, 128, 256), jnp.float32),
+            pltpu.VMEM((1024, 128), jnp.float32),
+        ],
+        input_output_aliases=aliases,
+        compiler_params=pltpu.CompilerParams(vmem_limit_bytes=VMEM_LIMIT),
+        cost_estimate=pl.CostEstimate(
+            flops=count * 4_000_000_000, bytes_accessed=count * 5_000_000, transcendentals=0
+        ),
+        name="shells_piece",
+    )(*operands)
+
+
+def on_device(pressure, legendre, radial):
+    frames, freq_dev, lat_dev, lon_count = pressure.shape
+    af_count = lax.axis_size("af")
+    sa_count = lax.axis_size("sa")
+    pairs_here = legendre.shape[0]
+    if (frames, freq_dev, lat_dev, af_count, sa_count) != (4, 8, 128, 4, 8):
+        return plain_on_device(pressure, legendre, radial)
+    devices = af_count * sa_count
+    owner_block = lax.axis_index("af") * sa_count + lax.axis_index("sa")
+    base = (owner_block * pairs_here).astype(jnp.int32).reshape(1)
+    factors = radial.reshape(LDEG * 32, 128)
+
+    lane = np.arange(256)
+    freq = (lane // 32 % 4) * 8 + lane % 8
+    rx = (lane // 128) * 4 + lane // 8 % 4
+    same = freq[:, None] == lane[None, :] % 32
+    pick = np.stack([same & (rx == k)[:, None] for k in range(8)])
+    pick = jnp.asarray(pick.astype(jnp.bfloat16))
+    flip = jnp.asarray(np.eye(128)[::-1].astype(jnp.bfloat16))
+
+    starts = [sum(CHUNKS[:i]) for i in range(len(CHUNKS))]
+    output = None
+    waiting = None
+    for i, (first, count) in enumerate(zip(starts, CHUNKS)):
+        table = jnp.asarray(table_rows(lon_count, devices, pairs_here, first, count))
+        spectra = dft(table, pressure)
+        if output is not None:
+            spectra, output = lax.optimization_barrier((spectra, output))
+        spread = spectra.reshape(devices, 4 * count * 32, 128)
+        piece = lax.all_to_all(spread, ("af", "sa"), split_axis=0, concat_axis=0, tiled=True)
+        piece = piece.reshape(devices, 2, 2, count, 32, 128)
+        if waiting is not None:
+            output = shells_piece(base, waiting[0], legendre, factors, pick, flip, output, *waiting[1:])
+        waiting = (piece, first, count)
+    output = shells_piece(base, waiting[0], legendre, factors, pick, flip, output, *waiting[1:])
+    return output.reshape(pairs_here, LDEG + 1, 2, frames, 128)
+
+
 def solution(mesh):
     return jax.shard_map(
         on_device,

time: 831 us -> 440 us (0.53)
  matrix products: 259 us -> 0 us
  Pallas kernels: 0 us -> 248 us
  local copies, waits for them, and re-layouts: 203 us -> 16.4 us
  waiting for transfers between devices: 307 us -> 153 us
  other arithmetic: 51.6 us -> 0 us
  starting transfers between devices: 7.6 us -> 21 us
    dot_general x3 -> x0, matrix products: 259 us -> none  [the longest x1 148 us: harmonics(): jnp.einsum('rkstxfj,kqj->krstxfq', folded, legendre, preferred_element_ty...]
    pallas_call x0 -> x10, Pallas kernels: none -> 248 us  [the longest x5 176 us: shells_piece(): pl.pallas_call(kernel, grid=(count,), in_specs=in_specs, out_specs=pl.Blo...]
    all_to_all x1 -> x5, waiting for transfers between devices: 307 us -> 153 us  [on_device(): lax.all_to_all(spread, ('af', 'sa'), split_axis=0, concat_axis=0, tiled=T...]
    gather x1 -> x0, local copies, waits for them, and re-layouts: 56.7 us -> none  [on_device(): factors = jnp.take(radial, degree.reshape(-1), axis=0)]
    convert_element_type x1 -> x0, local copies, waits for them, and re-layouts: 46.9 us -> none  [harmonics(): jnp.sum(products * select[:, None, :, :, None, None, :], axis=(2, 3))]
    another operation x1 -> x0, other arithmetic: 37.2 us -> none
    reshape x2 -> x0, local copies, waits for them, and re-layouts: 37 us -> none  [the longest x1 25.3 us: on_device(): sources.reshape(2, per_device, frame_count, af_count * freq_dev, sa_count...]
    transpose x1 -> x0, local copies, waits for them, and re-layouts: 32.2 us -> none  [on_device(): sources = jnp.transpose(sources, (2, 3, 4, 0, 5, 1, 6))]
  transfers between devices with their start and end apart: 1 -> 5, of which waited for: 1 -> 4; matrix products, arithmetic and copies ran while one was open for 7% -> 4% of each run, Pallas kernels for 0% -> 51%
where the time goes in v1:
time: 440 us; the launch traced here: 439 us
  Pallas kernels  248 us (56%)
  waiting for transfers between devices  153 us (35%)
  starting transfers between devices  21 us (5%)
  local copies, waits for them, and re-layouts  16.4 us (4%)
    pallas_call x5, Pallas kernels, shells_piece(): pl.pallas_call(kernel, grid=(count,), in_specs=in_specs, out_specs=pl.Blo...  176 us
    all_to_all x5, waiting for transfers between devices, on_device(): lax.all_to_all(spread, ('af', 'sa'), split_axis=0, concat_axis=0, tiled=T...  153 us
    pallas_call x5, Pallas kernels, dft(): pl.pallas_call(dft_kernel, grid=(4,), in_specs=[pl.BlockSpec((rows, lon_c...  71.6 us
    all_to_all x5, starting transfers between devices, on_device(): lax.all_to_all(spread, ('af', 'sa'), split_axis=0, concat_axis=0, tiled=T...  21 us
    unnamed x3, local copies, waits for them, and re-layouts  16.4 us
  transfers between devices with their start and end apart: 5, of which 4 were waited for; matrix products, arithmetic and copies ran while one was open for 4% of the time, Pallas kernels for 51%

profile of v1, /device:TPU:0, one launch (start us, length us, event | category | flops | bytes accessed | tf_op | source)
XLA Modules:
  0.0 438.9 jit_solution(6091678459654357198)
XLA Ops:
  0.0 10.7 %dft_piece.7 = bf16[256,32,128]{2,1,0:T(8,128)(2,1)} custom-call(bf16[256,2048]{1,0:T(8,128)(2,1)} %constant.28.clone.table_ref, bf16[4,8,128,2048]{3,2,1,0:T(8,128)(2,1)} %pressure_ref.9), custom_call_target="tpu_custom_call" | custom-call | flops 4294967296 | bytes 16777216 | tf_op jit(solution)/shard_map/dft_piece/pallas_call | solution.py:123
  10.7 7.4 %all-to-all-start = ((bf16[32,256,128]{2,1,0:T(8,128)(2,1)}), bf16[32,256,128]{2,1,0:T(8,128)(2,1)}, u32[]{:S(2)}, u32[]{:S(2)}) async-start(bf16[32,256,128]{2,1,0:T(8,128)(2,1)} %bitcast.18), calls=%async_computation | async-start | bytes 4194304 | tf_op jit(solution)/shard_map/all_to_all | solution.py:293
  18.2 18.6 %dft_piece.9 = bf16[640,32,128]{2,1,0:T(8,128)(2,1)} custom-call(bf16[640,2048]{1,0:T(8,128)(2,1)} %constant.29.clone.table_ref, bf16[4,8,128,2048]{3,2,1,0:T(8,128)(2,1)} %pressure_ref.9), custom_call_target="tpu_custom_call" | custom-call | flops 10737418240 | bytes 16777216 | tf_op jit(solution)/shard_map/dft_piece/pallas_call | solution.py:123
  36.8 31.5 %all-to-all-done = bf16[32,256,128]{2,1,0:T(8,128)(2,1)} async-done(((bf16[32,256,128]{2,1,0:T(8,128)(2,1)}), bf16[32,256,128]{2,1,0:T(8,128)(2,1)}, u32[]{:S(2)}, u32[]{:S(2)}) %all-to-all-start) | async-done | bytes 2097184 | tf_op jit(solution)/shard_map/all_to_all | solution.py:293
  68.3 3.6 all-to-all-start.2
  71.9 15.4 %copy.15.refs_2_ = bf16[16,1025,512]{2,1,0:T(8,128)(2,1)} copy(bf16[16,1025,512]{2,0,1:T(8,128)(2,1)} %param.11) | data formatting | bytes 33587200 | tf_op args[1]
  87.2 18.5 %dft_piece.6 = bf16[640,32,128]{2,1,0:T(8,128)(2,1)} custom-call(bf16[640,2048]{1,0:T(8,128)(2,1)} %constant.30.clone.table_ref, bf16[4,8,128,2048]{3,2,1,0:T(8,128)(2,1)} %pressure_ref.9), custom_call_target="tpu_custom_call" | custom-call | flops 10737418240 | bytes 16777216 | tf_op jit(solution)/shard_map/dft_piece/pallas_call | solution.py:123
  105.8 24.0 %shells_piece.5.refs_6_ = bf16[16,8200,128]{2,1,0:T(8,128)(2,1)} custom-call(s32[1]{0:T(128)} %bitcast.refs_0_, bf16[32,2,2,2,32,128]{5,4,3,2,1,0:T(8,128)(2,1)} %bitcast.2.refs_1_, bf16[16,1025,512]{2,1,0:T(8,128)(2,1)} %copy.15.refs_2_, bf16[32768,128]{1,0:T(8,128)(2,1)} %bitcast.13, bf16[8,256,256]{2,1,0:T(8,128)(2,1)} %constant.26.clone.refs_4_, ...), custom_call_target="tpu_custom_call" | custom-call | flops 8000000000 | bytes 10000000 | tf_op jit(solution)/shard_map/shells_piece/pallas_call | solution.py:243
  129.7 59.6 %all-to-all-done.2 = bf16[32,640,128]{2,1,0:T(8,128)(2,1)} async-done(((bf16[32,640,128]{2,1,0:T(8,128)(2,1)}), bf16[32,640,128]{2,1,0:T(8,128)(2,1)}, u32[]{:S(2)}, u32[]{:S(2)}) %all-to-all-start.2) | async-done | bytes 5242912 | tf_op jit(solution)/shard_map/all_to_all | solution.py:293
  189.4 3.8 all-to-all-start.1
  193.2 13.3 %dft_piece.8 = bf16[384,32,128]{2,1,0:T(8,128)(2,1)} custom-call(bf16[384,2048]{1,0:T(8,128)(2,1)} %constant.31.clone.table_ref, bf16[4,8,128,2048]{3,2,1,0:T(8,128)(2,1)} %pressure_ref.9), custom_call_target="tpu_custom_call" | custom-call | flops 6442450944 | bytes 16777216 | tf_op jit(solution)/shard_map/dft_piece/pallas_call | solution.py:123
  206.4 52.0 %shells_piece.6.refs_6_ = bf16[16,8200,128]{2,1,0:T(8,128)(2,1)} custom-call(s32[1]{0:T(128)} %bitcast.refs_0_, bf16[32,2,2,5,32,128]{5,4,3,2,1,0:T(8,128)(2,1)} %bitcast.7.refs_1_, bf16[16,1025,512]{2,1,0:T(8,128)(2,1)} %copy.15.refs_2_, bf16[32768,128]{1,0:T(8,128)(2,1)} %bitcast.14, ...), custom_call_target="tpu_custom_call", output_to_operand_aliasing={{}: (6, {})} | custom-call | flops 20000000000 | bytes 25000000 | tf_op jit(solution)/shard_map/shells_piece/pallas_call | solution.py:243
  258.4 52.1 %all-to-all-done.1 = bf16[32,640,128]{2,1,0:T(8,128)(2,1)} async-done(((bf16[32,640,128]{2,1,0:T(8,128)(2,1)}), bf16[32,640,128]{2,1,0:T(8,128)(2,1)}, u32[]{:S(2)}, u32[]{:S(2)}) %all-to-all-start.1) | async-done | bytes 5242912 | tf_op jit(solution)/shard_map/all_to_all | solution.py:293
  310.5 3.5 all-to-all-start.4
  314.1 10.5 %dft_piece.5 = bf16[128,32,128]{2,1,0:T(8,128)(2,1)} custom-call(bf16[128,2048]{1,0:T(8,128)(2,1)} %constant.32.clone.table_ref, bf16[4,8,128,2048]{3,2,1,0:T(8,128)(2,1)} %pressure_ref.9), custom_call_target="tpu_custom_call" | custom-call | flops 2147483648 | bytes 16777216 | tf_op jit(solution)/shard_map/dft_piece/pallas_call | solution.py:123
  324.6 51.8 %shells_piece.7.refs_6_ = bf16[16,8200,128]{2,1,0:T(8,128)(2,1)} custom-call(s32[1]{0:T(128)} %bitcast.refs_0_, bf16[32,2,2,5,32,128]{5,4,3,2,1,0:T(8,128)(2,1)} %bitcast.5.refs_1_, bf16[16,1025,512]{2,1,0:T(8,128)(2,1)} %copy.15.refs_2_, bf16[32768,128]{1,0:T(8,128)(2,1)} %bitcast.15, ...), custom_call_target="tpu_custom_call", output_to_operand_aliasing={{}: (6, {})} | custom-call | flops 20000000000 | bytes 25000000 | tf_op jit(solution)/shard_map/shells_piece/pallas_call | solution.py:243
  376.4 10.3 %all-to-all-done.4 = bf16[32,384,128]{2,1,0:T(8,128)(2,1)} async-done(((bf16[32,384,128]{2,1,0:T(8,128)(2,1)}), bf16[32,384,128]{2,1,0:T(8,128)(2,1)}, u32[]{:S(2)}, u32[]{:S(2)}) %all-to-all-start.4) | async-done | bytes 3145760 | tf_op jit(solution)/shard_map/all_to_all | solution.py:293
  386.7 2.6 all-to-all-start.3
  389.3 33.6 %shells_piece.8.refs_6_ = bf16[16,8200,128]{2,1,0:T(8,128)(2,1)} custom-call(s32[1]{0:T(128)} %bitcast.refs_0_, bf16[32,2,2,3,32,128]{5,4,3,2,1,0:T(8,128)(2,1)} %bitcast.11.refs_1_, bf16[16,1025,512]{2,1,0:T(8,128)(2,1)} %copy.15.refs_2_, bf16[32768,128]{1,0:T(8,128)(2,1)} %bitcast.16, ...), custom_call_target="tpu_custom_call", output_to_operand_aliasing={{}: (6, {})} | custom-call | flops 12000000000 | bytes 15000000 | tf_op jit(solution)/shard_map/shells_piece/pallas_call | solution.py:243
  423.0 0.0 all-to-all-done.3
  423.0 0.0 copy-start
  423.0 1.0 copy-done
  423.9 15.0 %shells_piece.9 = bf16[16,8200,128]{2,1,0:T(8,128)(2,1)} custom-call(s32[1]{0:T(128)} %bitcast.refs_0_, bf16[32,2,2,1,32,128]{5,4,3,2,1,0:T(8,128)(2,1)} %bitcast.21, bf16[16,1025,512]{2,1,0:T(8,128)(2,1)} %copy.15.refs_2_, bf16[32768,128]{1,0:T(8,128)(2,1)} %bitcast.17, ...), custom_call_target="tpu_custom_call", output_to_operand_aliasing={{}: (6, {})} | custom-call | flops 4000000000 | bytes 5000000 | tf_op jit(solution)/shard_map/shells_piece/pallas_call | solution.py:243
Async XLA Ops:
  10.7 57.5 %all-to-all-start = ((bf16[32,256,128]{2,1,0:T(8,128)(2,1)}), bf16[32,256,128]{2,1,0:T(8,128)(2,1)}, u32[]{:S(2)}, u32[]{:S(2)}) async-start(bf16[32,256,128]{2,1,0:T(8,128)(2,1)} %bitcast.18), calls=%async_computation | async-start | bytes 4194304 | tf_op jit(solution)/shard_map/all_to_all | solution.py:293
  68.3 121.1 %all-to-all-start.2 = ((bf16[32,640,128]{2,1,0:T(8,128)(2,1)}), bf16[32,640,128]{2,1,0:T(8,128)(2,1)}, u32[]{:S(2)}, u32[]{:S(2)}) async-start(bf16[32,640,128]{2,1,0:T(8,128)(2,1)} %bitcast.19), calls=%async_computation.2 | async-start | bytes 10485760 | tf_op jit(solution)/shard_map/all_to_all | solution.py:293
  189.4 121.1 %all-to-all-start.1 = ((bf16[32,640,128]{2,1,0:T(8,128)(2,1)}), bf16[32,640,128]{2,1,0:T(8,128)(2,1)}, u32[]{:S(2)}, u32[]{:S(2)}) async-start(bf16[32,640,128]{2,1,0:T(8,128)(2,1)} %bitcast.20), calls=%async_computation.1 | async-start | bytes 10485760 | tf_op jit(solution)/shard_map/all_to_all | solution.py:293
  310.5 76.2 %all-to-all-start.4 = ((bf16[32,384,128]{2,1,0:T(8,128)(2,1)}), bf16[32,384,128]{2,1,0:T(8,128)(2,1)}, u32[]{:S(2)}, u32[]{:S(2)}) async-start(bf16[32,384,128]{2,1,0:T(8,128)(2,1)} %bitcast.23), calls=%async_computation.4 | async-start | bytes 6291456 | tf_op jit(solution)/shard_map/all_to_all | solution.py:293
  386.7 36.3 %all-to-all-start.3 = ((bf16[32,128,128]{2,1,0:T(8,128)(2,1)}), bf16[32,128,128]{2,1,0:T(8,128)(2,1)S(1)}, u32[]{:S(2)}, u32[]{:S(2)}) async-start(bf16[32,128,128]{2,1,0:T(8,128)(2,1)} %bitcast.22), calls=%async_computation.3 | async-start | bytes 2097152 | tf_op jit(solution)/shard_map/all_to_all | solution.py:293
  423.0 1.0 copy-start

commit v2 on v1

--- a/solution.py
+++ b/solution.py
@@ -9,7 +9,8 @@
 from jax.sharding import PartitionSpec as P
 
 LDEG = 1024
-CHUNKS = (2, 5, 5, 3, 1)
+CHUNKS = (1, 10, 4, 1)
+TILE = 512
 VMEM_LIMIT = 62 * 1024 * 1024
 
 
@@ -139,23 +140,18 @@
 
 
 def shells_kernel(first, *refs):
-    base_ref, recv_ref, leg_ref, rad_ref, pick_ref, flip_ref = refs[:6]
+    base_ref, recv_ref, leg_ref, rad_ref, pick_ref, turn_ref = refs[:6]
     out_ref, both_ref, harm_ref, copies_ref, result_ref = refs[-5:]
     pair = base_ref[0] + first + pl.program_id(0)
     bound = LDEG - pair
 
     for s in range(4):
-        lanes = slice(128 * s, 128 * s + 128)
         for seg in range(2):
-            mirrored = []
-            for r in range(2):
-                for a in range(4):
-                    row = 128 * r + 32 * a
-                    both_ref[seg, row : row + 32, lanes] = recv_ref[8 * a + s, r, seg, 0]
-                    mirrored.append(recv_ref[8 * a + 7 - s, r, seg, 0])
-            mirrored = jnp.concatenate(mirrored, axis=0)
-            turned = jnp.dot(mirrored, flip_ref[...], preferred_element_type=jnp.float32)
-            both_ref[seg, 256:512, lanes] = turned.astype(jnp.bfloat16)
+            for half, sa in ((0, s), (1, 7 - s)):
+                rows = [recv_ref[8 * a + sa, r, seg, 0] for r in range(2) for a in range(4)]
+                turned = dot_t(turn_ref[half], jnp.concatenate(rows, axis=0))
+                lanes = slice(256 * half, 256 * half + 256)
+                both_ref[seg, 128 * s : 128 * s + 128, lanes] = turned.astype(jnp.bfloat16)
 
     own_q = (
         lax.broadcasted_iota(jnp.int32, (64, 256), 1) // 32
@@ -163,7 +159,7 @@
     )
 
     def legendre_rows(rows, start, seg):
-        product = dot_t(rows, both_ref[seg])
+        product = jnp.dot(rows, both_ref[seg], preferred_element_type=jnp.float32)
         q = start + lax.broadcasted_iota(jnp.int32, (rows.shape[0], 256), 0)
         parity = (q + seg * pair) % 2
         north, south = product[:, :256], product[:, 256:]
@@ -189,36 +185,45 @@
         for rx in range(8):
             result_ref[pl.ds(64 * block + rx, 8, stride=8), :] = result[8 * rx : 8 * rx + 8]
 
-    @pl.loop(0, 8)
-    def _(tile):
-        start = pl.multiple_of(tile * 128, 128)
-        rows = leg_ref[0, pl.ds(start, 128), :]
+    def columns(start, rows, slabs):
+        count = rows.shape[0]
 
         @pl.when(start < bound)
         def _():
             _, harm = legendre_rows(rows, start, 0)
-            harm_ref[...] = harm
-
-        @pl.when(start + 128 > bound)
+            harm_ref[0:count] = harm
+
+        @pl.when(start + count > bound)
         def _():
             q, harm = legendre_rows(rows, start, 1)
-            harm_ref[...] = jnp.where(q >= bound, harm, harm_ref[...])
-
-        fill_copies(harm_ref[...])
-        for block in range(16):
-            slab = [factors_at(degree(start + 8 * block + k)) for k in range(8)]
-            radial_block(block, jnp.concatenate(slab, axis=0))
+            harm_ref[0:count] = jnp.where(q >= bound, harm, harm_ref[0:count])
+
+        fill_copies(harm_ref[0:count])
+        for block, slab in enumerate(slabs):
+            radial_block(block, jnp.concatenate(slab(), axis=0))
         at = pl.multiple_of(start * 8, 1024)
-        out_ref[0, pl.ds(at, 1024), :] = result_ref[...].astype(jnp.bfloat16)
-
-    rows = jnp.broadcast_to(leg_ref[0, LDEG : LDEG + 1, :].astype(jnp.float32), (16, 512))
-    _, harm = legendre_rows(rows.astype(jnp.bfloat16), LDEG, 1)
-    fill_copies(jnp.broadcast_to(harm[0:1], (16, 256)))
-    radial_block(0, jnp.concatenate([factors_at(LDEG - 1)] * 8, axis=0))
-    out_ref[0, 8 * LDEG : 8 * LDEG + 8, :] = result_ref[0:8].astype(jnp.bfloat16)
-
-
-def shells_piece(base, received, legendre, radial, pick, flip, output, first, count):
+        out_rows = min(8 * count, 8 * (LDEG + 1) - 8 * (LDEG - TILE))
+        out_ref[0, pl.ds(at, out_rows), :] = result_ref[0:out_rows].astype(jnp.bfloat16)
+
+    def slab_of(start, block):
+        return lambda: [factors_at(degree(start + 8 * block + k)) for k in range(8)]
+
+    @pl.loop(0, LDEG // TILE - 1)
+    def _(tile):
+        start = pl.multiple_of(tile * TILE, TILE)
+        rows = leg_ref[0, pl.ds(start, TILE), :]
+        columns(start, rows, [slab_of(start, block) for block in range(TILE // 8)])
+
+    start = LDEG - TILE
+    last = leg_ref[0, LDEG : LDEG + 1, :].astype(jnp.float32)
+    last = jnp.broadcast_to(last, (16, 512)).astype(jnp.bfloat16)
+    rows = jnp.concatenate([leg_ref[0, start:LDEG, :], last], axis=0)
+    slabs = [slab_of(start, block) for block in range(TILE // 8)]
+    slabs.append(lambda: [factors_at(LDEG - 1)] * 8)
+    columns(start, rows, slabs)
+
+
+def shells_piece(base, received, legendre, radial, pick, turn, output, first, count):
     pairs_here = legendre.shape[0]
     rows = 8 * (LDEG + 1)
     once = pl.Buffered(1)
@@ -228,9 +233,9 @@
         pl.BlockSpec((1, LDEG + 1, 512), lambda i: (first + i, 0, 0)),
         pl.BlockSpec(radial.shape, lambda i: (0, 0), pipeline_mode=once),
         pl.BlockSpec((8, 256, 256), lambda i: (0, 0, 0)),
-        pl.BlockSpec((128, 128), lambda i: (0, 0)),
+        pl.BlockSpec((2, 128, 128), lambda i: (0, 0, 0)),
     ]
-    operands = [base, received, legendre, radial, pick, flip]
+    operands = [base, received, legendre, radial, pick, turn]
     aliases = {}
     if output is not None:
         in_specs.append(pl.BlockSpec(memory_space=pl.ANY))
@@ -248,9 +253,9 @@
         out_shape=jax.ShapeDtypeStruct((pairs_here, rows, 128), jnp.bfloat16),
         scratch_shapes=[
             pltpu.VMEM((2, 512, 512), jnp.bfloat16),
-            pltpu.VMEM((128, 256), jnp.float32),
-            pltpu.VMEM((8, 128, 256), jnp.float32),
-            pltpu.VMEM((1024, 128), jnp.float32),
+            pltpu.VMEM((TILE + 16, 256), jnp.float32),
+            pltpu.VMEM((8, TILE + 16, 256), jnp.float32),
+            pltpu.VMEM((8 * TILE + 128, 128), jnp.float32),
         ],
         input_output_aliases=aliases,
         compiler_params=pltpu.CompilerParams(vmem_limit_bytes=VMEM_LIMIT),
@@ -279,7 +284,7 @@
     same = freq[:, None] == lane[None, :] % 32
     pick = np.stack([same & (rx == k)[:, None] for k in range(8)])
     pick = jnp.asarray(pick.astype(jnp.bfloat16))
-    flip = jnp.asarray(np.eye(128)[::-1].astype(jnp.bfloat16))
+    turn = jnp.asarray(np.stack([np.eye(128), np.eye(128)[::-1]]).astype(jnp.bfloat16))
 
     starts = [sum(CHUNKS[:i]) for i in range(len(CHUNKS))]
     output = None
@@ -293,9 +298,9 @@
         piece = lax.all_to_all(spread, ("af", "sa"), split_axis=0, concat_axis=0, tiled=True)
         piece = piece.reshape(devices, 2, 2, count, 32, 128)
         if waiting is not None:
-            output = shells_piece(base, waiting[0], legendre, factors, pick, flip, output, *waiting[1:])
+            output = shells_piece(base, waiting[0], legendre, factors, pick, turn, output, *waiting[1:])
         waiting = (piece, first, count)
-    output = shells_piece(base, waiting[0], legendre, factors, pick, flip, output, *waiting[1:])
+    output = shells_piece(base, waiting[0], legendre, factors, pick, turn, output, *waiting[1:])
     return output.reshape(pairs_here, LDEG + 1, 2, frames, 128)
 
 

time: 440 us -> 432 us (0.982)
  Pallas kernels: 248 us -> 189 us
  waiting for transfers between devices: 153 us -> 206 us
    pallas_call x5 -> x4, Pallas kernels: 176 us -> 118 us  [shells_piece(): pl.pallas_call(kernel, grid=(count,), in_specs=in_specs, out_specs=pl.Blo...]
    all_to_all x5 -> x4, waiting for transfers between devices: 153 us -> 206 us  [on_device(): lax.all_to_all(spread, ('af', 'sa'), split_axis=0, concat_axis=0, tiled=T...]
    all_to_all x5 -> x4, starting transfers between devices: 21 us -> 19.7 us  [on_device(): lax.all_to_all(spread, ('af', 'sa'), split_axis=0, concat_axis=0, tiled=T...]
    pallas_call x5 -> x4, Pallas kernels: 71.6 us -> 70.4 us  [dft(): pl.pallas_call(dft_kernel, grid=(4,), in_specs=[pl.BlockSpec((rows, lon_c...]
    unnamed x3 -> x5, local copies, waits for them, and re-layouts: 16.4 us -> 16.4 us
  transfers between devices with their start and end apart: 5 -> 4, of which waited for: 4 -> 2; matrix products, arithmetic and copies ran while one was open for 4% -> 4% of each run, Pallas kernels for 51% -> 39%
where the time goes in v2:
time: 432 us; the launch traced here: 431 us
  waiting for transfers between devices  206 us (48%)
  Pallas kernels  189 us (44%)
  starting transfers between devices  19.7 us (5%)
  local copies, waits for them, and re-layouts  16.4 us (4%)
    all_to_all x4, waiting for transfers between devices, on_device(): lax.all_to_all(spread, ('af', 'sa'), split_axis=0, concat_axis=0, tiled=T...  206 us
    pallas_call x4, Pallas kernels, shells_piece(): pl.pallas_call(kernel, grid=(count,), in_specs=in_specs, out_specs=pl.Blo...  118 us
    pallas_call x4, Pallas kernels, dft(): pl.pallas_call(dft_kernel, grid=(4,), in_specs=[pl.BlockSpec((rows, lon_c...  70.4 us
    all_to_all x4, starting transfers between devices, on_device(): lax.all_to_all(spread, ('af', 'sa'), split_axis=0, concat_axis=0, tiled=T...  19.7 us
    unnamed x5, local copies, waits for them, and re-layouts  16.4 us
  transfers between devices with their start and end apart: 4, of which 2 were waited for; matrix products, arithmetic and copies ran while one was open for 4% of the time, Pallas kernels for 39%

profile of v2, /device:TPU:0, one launch (start us, length us, event | category | flops | bytes accessed | tf_op | source)
XLA Modules:
  0.0 431.0 jit_solution(9795205872541143196)
XLA Ops:
  0.0 10.5 %dft_piece.7 = bf16[128,32,128]{2,1,0:T(8,128)(2,1)} custom-call(bf16[128,2048]{1,0:T(8,128)(2,1)} %constant.26.clone.table_ref, bf16[4,8,128,2048]{3,2,1,0:T(8,128)(2,1)} %pressure_ref.7), custom_call_target="tpu_custom_call" | custom-call | flops 2147483648 | bytes 16777216 | tf_op jit(solution)/shard_map/dft_piece/pallas_call | solution.py:124
  10.5 7.3 %all-to-all-start.1 = ((bf16[32,128,128]{2,1,0:T(8,128)(2,1)}), bf16[32,128,128]{2,1,0:T(8,128)(2,1)S(1)}, u32[]{:S(2)}, u32[]{:S(2)}) async-start(bf16[32,128,128]{2,1,0:T(8,128)(2,1)} %bitcast.19), calls=%async_computation.1 | async-start | bytes 2097152 | tf_op jit(solution)/shard_map/all_to_all | solution.py:298
  17.8 33.6 %dft_piece.5 = bf16[1280,32,128]{2,1,0:T(8,128)(2,1)} custom-call(bf16[1280,2048]{1,0:T(8,128)(2,1)} %constant.27.clone.table_ref, bf16[4,8,128,2048]{3,2,1,0:T(8,128)(2,1)} %pressure_ref.7), custom_call_target="tpu_custom_call" | custom-call | flops 21474836480 | bytes 16777216 | tf_op jit(solution)/shard_map/dft_piece/pallas_call | solution.py:124
  51.4 0.0 all-to-all-done.1
  51.4 0.0 copy-start
  51.4 5.9 %all-to-all-start = ((bf16[32,1280,128]{2,1,0:T(8,128)(2,1)}), bf16[32,1280,128]{2,1,0:T(8,128)(2,1)}, u32[]{:S(2)}, u32[]{:S(2)}) async-start(bf16[32,1280,128]{2,1,0:T(8,128)(2,1)} %bitcast.15), calls=%async_computation | async-start | bytes 20971520 | tf_op jit(solution)/shard_map/all_to_all | solution.py:298
  57.4 15.4 %copy.14.refs_2_ = bf16[16,1025,512]{2,1,0:T(8,128)(2,1)} copy(bf16[16,1025,512]{2,0,1:T(8,128)(2,1)} %param.10) | data formatting | bytes 33587200 | tf_op args[1]
  72.8 0.0 copy-done
  72.8 15.7 %dft_piece.6 = bf16[512,32,128]{2,1,0:T(8,128)(2,1)} custom-call(bf16[512,2048]{1,0:T(8,128)(2,1)} %constant.28.clone.table_ref, bf16[4,8,128,2048]{3,2,1,0:T(8,128)(2,1)} %pressure_ref.7), custom_call_target="tpu_custom_call" | custom-call | flops 8589934592 | bytes 16777216 | tf_op jit(solution)/shard_map/dft_piece/pallas_call | solution.py:124
  88.5 11.8 %shells_piece.4.refs_6_ = bf16[16,8200,128]{2,1,0:T(8,128)(2,1)} custom-call(s32[1]{0:T(128)} %bitcast.refs_0_, bf16[32,2,2,1,32,128]{5,4,3,2,1,0:T(8,128)(2,1)} %bitcast.16, bf16[16,1025,512]{2,1,0:T(8,128)(2,1)} %copy.14.refs_2_, bf16[32768,128]{1,0:T(8,128)(2,1)} %bitcast.11, bf16[8,256,256]{2,1,0:T(8,128)(2,1)} %constant.24.clone.refs_4_, ...), custom_call_target="tpu_custom_call" | custom-call | flops 4000000000 | bytes 5000000 | tf_op jit(solution)/shard_map/shells_piece/pallas_call | solution.py:248
  100.3 186.9 %all-to-all-done = bf16[32,1280,128]{2,1,0:T(8,128)(2,1)} async-done(((bf16[32,1280,128]{2,1,0:T(8,128)(2,1)}), bf16[32,1280,128]{2,1,0:T(8,128)(2,1)}, u32[]{:S(2)}, u32[]{:S(2)}) %all-to-all-start) | async-done | bytes 10485792 | tf_op jit(solution)/shard_map/all_to_all | solution.py:298
  287.2 3.6 all-to-all-start.3
  290.8 10.5 %dft_piece.4 = bf16[128,32,128]{2,1,0:T(8,128)(2,1)} custom-call(bf16[128,2048]{1,0:T(8,128)(2,1)} %constant.29.clone.table_ref, bf16[4,8,128,2048]{3,2,1,0:T(8,128)(2,1)} %pressure_ref.7), custom_call_target="tpu_custom_call" | custom-call | flops 2147483648 | bytes 16777216 | tf_op jit(solution)/shard_map/dft_piece/pallas_call | solution.py:124
  301.3 65.3 %shells_piece.5.refs_6_ = bf16[16,8200,128]{2,1,0:T(8,128)(2,1)} custom-call(s32[1]{0:T(128)} %bitcast.refs_0_, bf16[32,2,2,10,32,128]{5,4,3,2,1,0:T(8,128)(2,1)} %bitcast.2.refs_1_, bf16[16,1025,512]{2,1,0:T(8,128)(2,1)} %copy.14.refs_2_, bf16[32768,128]{1,0:T(8,128)(2,1)} %bitcast.12, ...), custom_call_target="tpu_custom_call", output_to_operand_aliasing={{}: (6, {})} | custom-call | flops 40000000000 | bytes 50000000 | tf_op jit(solution)/shard_map/shells_piece/pallas_call | solution.py:248
  366.6 19.2 %all-to-all-done.3 = bf16[32,512,128]{2,1,0:T(8,128)(2,1)} async-done(((bf16[32,512,128]{2,1,0:T(8,128)(2,1)}), bf16[32,512,128]{2,1,0:T(8,128)(2,1)}, u32[]{:S(2)}, u32[]{:S(2)}) %all-to-all-start.3) | async-done | bytes 4194336 | tf_op jit(solution)/shard_map/all_to_all | solution.py:298
  385.9 2.9 all-to-all-start.2
  388.7 29.5 %shells_piece.6.refs_6_ = bf16[16,8200,128]{2,1,0:T(8,128)(2,1)} custom-call(s32[1]{0:T(128)} %bitcast.refs_0_, bf16[32,2,2,4,32,128]{5,4,3,2,1,0:T(8,128)(2,1)} %bitcast.9.refs_1_, bf16[16,1025,512]{2,1,0:T(8,128)(2,1)} %copy.14.refs_2_, bf16[32768,128]{1,0:T(8,128)(2,1)} %bitcast.13, ...), custom_call_target="tpu_custom_call", output_to_operand_aliasing={{}: (6, {})} | custom-call | flops 16000000000 | bytes 20000000 | tf_op jit(solution)/shard_map/shells_piece/pallas_call | solution.py:248
  418.3 0.0 all-to-all-done.2
  418.3 0.0 copy-start.1
  418.3 1.0 copy-done.1
  419.3 11.7 %shells_piece.7 = bf16[16,8200,128]{2,1,0:T(8,128)(2,1)} custom-call(s32[1]{0:T(128)} %bitcast.refs_0_, bf16[32,2,2,1,32,128]{5,4,3,2,1,0:T(8,128)(2,1)} %bitcast.17, bf16[16,1025,512]{2,1,0:T(8,128)(2,1)} %copy.14.refs_2_, bf16[32768,128]{1,0:T(8,128)(2,1)} %bitcast.14, ...), custom_call_target="tpu_custom_call", output_to_operand_aliasing={{}: (6, {})} | custom-call | flops 4000000000 | bytes 5000000 | tf_op jit(solution)/shard_map/shells_piece/pallas_call | solution.py:248
Async XLA Ops:
  10.5 40.9 %all-to-all-start.1 = ((bf16[32,128,128]{2,1,0:T(8,128)(2,1)}), bf16[32,128,128]{2,1,0:T(8,128)(2,1)S(1)}, u32[]{:S(2)}, u32[]{:S(2)}) async-start(bf16[32,128,128]{2,1,0:T(8,128)(2,1)} %bitcast.19), calls=%async_computation.1 | async-start | bytes 2097152 | tf_op jit(solution)/shard_map/all_to_all | solution.py:298
  51.4 21.3 %copy-start = (bf16[32,128,128]{2,1,0:T(8,128)(2,1)}, bf16[32,128,128]{2,1,0:T(8,128)(2,1)S(1)}, u32[]{:S(2)}) copy-start(bf16[32,128,128]{2,1,0:T(8,128)(2,1)S(1)} %all-to-all-done.1) | copy-start | bytes 3145732
  51.4 235.8 %all-to-all-start = ((bf16[32,1280,128]{2,1,0:T(8,128)(2,1)}), bf16[32,1280,128]{2,1,0:T(8,128)(2,1)}, u32[]{:S(2)}, u32[]{:S(2)}) async-start(bf16[32,1280,128]{2,1,0:T(8,128)(2,1)} %bitcast.15), calls=%async_computation | async-start | bytes 20971520 | tf_op jit(solution)/shard_map/all_to_all | solution.py:298
  287.2 98.7 %all-to-all-start.3 = ((bf16[32,512,128]{2,1,0:T(8,128)(2,1)}), bf16[32,512,128]{2,1,0:T(8,128)(2,1)}, u32[]{:S(2)}, u32[]{:S(2)}) async-start(bf16[32,512,128]{2,1,0:T(8,128)(2,1)} %bitcast.20), calls=%async_computation.3 | async-start | bytes 8388608 | tf_op jit(solution)/shard_map/all_to_all | solution.py:298
  385.9 32.4 %all-to-all-start.2 = ((bf16[32,128,128]{2,1,0:T(8,128)(2,1)}), bf16[32,128,128]{2,1,0:T(8,128)(2,1)S(1)}, u32[]{:S(2)}, u32[]{:S(2)}) async-start(bf16[32,128,128]{2,1,0:T(8,128)(2,1)} %bitcast.18), calls=%async_computation.2 | async-start | bytes 2097152 | tf_op jit(solution)/shard_map/all_to_all | solution.py:298
  418.3 1.0 copy-start.1

commit v3 on v2

--- a/solution.py
+++ b/solution.py
@@ -9,9 +9,9 @@
 from jax.sharding import PartitionSpec as P
 
 LDEG = 1024
-CHUNKS = (1, 10, 4, 1)
+CHUNKS = (2, 10, 3, 1)
 TILE = 512
-VMEM_LIMIT = 62 * 1024 * 1024
+VMEM_LIMIT = 63 * 1024 * 1024
 
 
 def order_of_column(column_count):
@@ -140,10 +140,24 @@
 
 
 def shells_kernel(first, *refs):
-    base_ref, recv_ref, leg_ref, rad_ref, pick_ref, turn_ref = refs[:6]
-    out_ref, both_ref, harm_ref, copies_ref, result_ref = refs[-5:]
+    base_ref, recv_ref, leg_ref, rad_hbm_ref, pick_ref, turn_ref = refs[:6]
+    out_ref, both_ref, harm_ref, copies_ref, result_ref, rad_ref, rad_sem = refs[-7:]
     pair = base_ref[0] + first + pl.program_id(0)
     bound = LDEG - pair
+    quarter = rad_ref.shape[0] // 4
+    radial_copies = [
+        pltpu.make_async_copy(
+            rad_hbm_ref.at[pl.ds(k * quarter, quarter)],
+            rad_ref.at[pl.ds(k * quarter, quarter)],
+            rad_sem.at[k],
+        )
+        for k in range(4)
+    ]
+
+    @pl.when(pl.program_id(0) == 0)
+    def _():
+        for copy in radial_copies:
+            copy.start()
 
     for s in range(4):
         for seg in range(2):
@@ -154,8 +168,8 @@
                 both_ref[seg, 128 * s : 128 * s + 128, lanes] = turned.astype(jnp.bfloat16)
 
     own_q = (
-        lax.broadcasted_iota(jnp.int32, (64, 256), 1) // 32
-        == lax.broadcasted_iota(jnp.int32, (64, 256), 0) % 8
+        lax.broadcasted_iota(jnp.int32, (1, 8, 256), 2) // 32
+        == lax.broadcasted_iota(jnp.int32, (1, 8, 256), 1)
     )
 
     def legendre_rows(rows, start, seg):
@@ -172,20 +186,24 @@
         return rad_ref[pl.ds(pl.multiple_of(degree_here * 32, 32), 32), :]
 
     def fill_copies(harm):
+        count = harm.shape[0]
         harm = harm.astype(jnp.bfloat16)
         for rx in range(8):
-            copies_ref[rx, 0 : harm.shape[0]] = jnp.dot(
-                harm, pick_ref[rx], preferred_element_type=jnp.float32
-            )
+            copies = jnp.dot(harm, pick_ref[rx], preferred_element_type=jnp.float32)
+            own = jnp.where(own_q, copies.reshape(count // 8, 8, 256), 0.0)
+            copies_ref[rx, 0:count] = own.reshape(count, 256).astype(jnp.bfloat16)
 
     def radial_block(block, slab):
-        rows = [copies_ref[rx, 8 * block : 8 * block + 8] for rx in range(8)]
-        diagonal = jnp.where(own_q, jnp.concatenate(rows, axis=0), 0.0).astype(jnp.bfloat16)
-        result = jnp.dot(diagonal, slab, preferred_element_type=jnp.float32)
+        rows = [copies_ref[rx, 16 * block : 16 * block + 16] for rx in range(8)]
+        rows = jnp.concatenate(rows, axis=0)
+        result = jnp.dot(rows, slab, preferred_element_type=jnp.float32)
         for rx in range(8):
-            result_ref[pl.ds(64 * block + rx, 8, stride=8), :] = result[8 * rx : 8 * rx + 8]
-
-    def columns(start, rows, slabs):
+            for half in range(2):
+                at = 128 * block + 64 * half + rx
+                part = result[16 * rx + 8 * half :, 128 * half : 128 * half + 128]
+                result_ref[pl.ds(at, 8, stride=8), :] = part[:8]
+
+    def columns(start, rows, slabs, first_tile):
         count = rows.shape[0]
 
         @pl.when(start < bound)
@@ -199,39 +217,47 @@
             harm_ref[0:count] = jnp.where(q >= bound, harm, harm_ref[0:count])
 
         fill_copies(harm_ref[0:count])
+        if first_tile:
+
+            @pl.when(pl.program_id(0) == 0)
+            def _():
+                for copy in radial_copies:
+                    copy.wait()
+
         for block, slab in enumerate(slabs):
-            radial_block(block, jnp.concatenate(slab(), axis=0))
-        at = pl.multiple_of(start * 8, 1024)
+            radial_block(block, slab())
         out_rows = min(8 * count, 8 * (LDEG + 1) - 8 * (LDEG - TILE))
-        out_ref[0, pl.ds(at, out_rows), :] = result_ref[0:out_rows].astype(jnp.bfloat16)
+        out_ref[0, 8 * start : 8 * start + out_rows, :] = result_ref[0:out_rows].astype(jnp.bfloat16)
 
     def slab_of(start, block):
-        return lambda: [factors_at(degree(start + 8 * block + k)) for k in range(8)]
-
-    @pl.loop(0, LDEG // TILE - 1)
-    def _(tile):
-        start = pl.multiple_of(tile * TILE, TILE)
-        rows = leg_ref[0, pl.ds(start, TILE), :]
-        columns(start, rows, [slab_of(start, block) for block in range(TILE // 8)])
+        def slab():
+            q = start + 16 * block
+            halves = [[factors_at(degree(q + 8 * half + k)) for k in range(8)] for half in range(2)]
+            return jnp.concatenate([jnp.concatenate(h, axis=0) for h in halves], axis=1)
+
+        return slab
+
+    for start in range(0, LDEG - TILE, TILE):
+        rows = leg_ref[0, start : start + TILE, :]
+        columns(start, rows, [slab_of(start, block) for block in range(TILE // 16)], start == 0)
 
     start = LDEG - TILE
     last = leg_ref[0, LDEG : LDEG + 1, :].astype(jnp.float32)
     last = jnp.broadcast_to(last, (16, 512)).astype(jnp.bfloat16)
     rows = jnp.concatenate([leg_ref[0, start:LDEG, :], last], axis=0)
-    slabs = [slab_of(start, block) for block in range(TILE // 8)]
-    slabs.append(lambda: [factors_at(LDEG - 1)] * 8)
-    columns(start, rows, slabs)
+    slabs = [slab_of(start, block) for block in range(TILE // 16)]
+    slabs.append(lambda: jnp.tile(factors_at(LDEG - 1), (8, 2)))
+    columns(start, rows, slabs, False)
 
 
 def shells_piece(base, received, legendre, radial, pick, turn, output, first, count):
     pairs_here = legendre.shape[0]
     rows = 8 * (LDEG + 1)
-    once = pl.Buffered(1)
     in_specs = [
         pl.BlockSpec(memory_space=pltpu.SMEM),
         pl.BlockSpec((32, 2, 2, 1, 32, 128), lambda i: (0, 0, 0, i, 0, 0)),
         pl.BlockSpec((1, LDEG + 1, 512), lambda i: (first + i, 0, 0)),
-        pl.BlockSpec(radial.shape, lambda i: (0, 0), pipeline_mode=once),
+        pl.BlockSpec(memory_space=pl.ANY),
         pl.BlockSpec((8, 256, 256), lambda i: (0, 0, 0)),
         pl.BlockSpec((2, 128, 128), lambda i: (0, 0, 0)),
     ]
@@ -254,8 +280,10 @@
         scratch_shapes=[
             pltpu.VMEM((2, 512, 512), jnp.bfloat16),
             pltpu.VMEM((TILE + 16, 256), jnp.float32),
-            pltpu.VMEM((8, TILE + 16, 256), jnp.float32),
+            pltpu.VMEM((8, TILE + 16, 256), jnp.bfloat16),
             pltpu.VMEM((8 * TILE + 128, 128), jnp.float32),
+            pltpu.VMEM(radial.shape, jnp.bfloat16),
+            pltpu.SemaphoreType.DMA((4,)),
         ],
         input_output_aliases=aliases,
         compiler_params=pltpu.CompilerParams(vmem_limit_bytes=VMEM_LIMIT),
@@ -287,14 +315,19 @@
     turn = jnp.asarray(np.stack([np.eye(128), np.eye(128)[::-1]]).astype(jnp.bfloat16))
 
     starts = [sum(CHUNKS[:i]) for i in range(len(CHUNKS))]
+    tables = [
+        jnp.asarray(table_rows(lon_count, devices, pairs_here, first, count))
+        for first, count in zip(starts, CHUNKS)
+    ]
+    spectra = [dft(table, pressure) for table in tables]
     output = None
     waiting = None
     for i, (first, count) in enumerate(zip(starts, CHUNKS)):
-        table = jnp.asarray(table_rows(lon_count, devices, pairs_here, first, count))
-        spectra = dft(table, pressure)
         if output is not None:
-            spectra, output = lax.optimization_barrier((spectra, output))
-        spread = spectra.reshape(devices, 4 * count * 32, 128)
+            spectra[i], output = lax.optimization_barrier((spectra[i], output))
+        if i == len(CHUNKS) - 2:
+            spectra[i:] = lax.optimization_barrier(tuple(spectra[i:]))
+        spread = spectra[i].reshape(devices, 4 * count * 32, 128)
         piece = lax.all_to_all(spread, ("af", "sa"), split_axis=0, concat_axis=0, tiled=True)
         piece = piece.reshape(devices, 2, 2, count, 32, 128)
         if waiting is not None:

time: 432 us -> 421 us (0.975)
  waiting for transfers between devices: 206 us -> 200 us
    all_to_all x4, waiting for transfers between devices: 206 us -> 200 us  [on_device(): lax.all_to_all(spread, ('af', 'sa'), split_axis=0, concat_axis=0, tiled=T...]
    unnamed x5 -> x1, local copies, waits for them, and re-layouts: 16.4 us -> 15.4 us
  transfers between devices with their start and end apart: 4 -> 4, of which waited for: 2 -> 4; matrix products, arithmetic and copies ran while one was open for 4% -> 4% of each run, Pallas kernels for 39% -> 39%
where the time goes in v3:
time: 421 us; the launch traced here: 420 us
  waiting for transfers between devices  200 us (48%)
  Pallas kernels  186 us (44%)
  starting transfers between devices  18.4 us (4%)
  local copies, waits for them, and re-layouts  15.4 us (4%)
    all_to_all x4, waiting for transfers between devices, on_device(): lax.all_to_all(spread, ('af', 'sa'), split_axis=0, concat_axis=0, tiled=T...  200 us
    pallas_call x4, Pallas kernels, shells_piece(): pl.pallas_call(kernel, grid=(count,), in_specs=in_specs, out_specs=pl.Blo...  118 us
    pallas_call x4, Pallas kernels, dft(): pl.pallas_call(dft_kernel, grid=(4,), in_specs=[pl.BlockSpec((rows, lon_c...  68 us
    all_to_all x4, starting transfers between devices, on_device(): lax.all_to_all(spread, ('af', 'sa'), split_axis=0, concat_axis=0, tiled=T...  18.4 us
    unnamed x1, local copies, waits for them, and re-layouts  15.4 us
  transfers between devices with their start and end apart: 4, of which 4 were waited for; matrix products, arithmetic and copies ran while one was open for 4% of the time, Pallas kernels for 39%

profile of v3, /device:TPU:0, one launch (start us, length us, event | category | flops | bytes accessed | tf_op | source)
XLA Modules:
  0.0 420.3 jit_solution(11116389030092885375)
XLA Ops:
  0.0 10.7 %dft_piece.5 = bf16[256,32,128]{2,1,0:T(8,128)(2,1)} custom-call(bf16[256,2048]{1,0:T(8,128)(2,1)} %constant.26.clone.table_ref, bf16[4,8,128,2048]{3,2,1,0:T(8,128)(2,1)} %pressure_ref.7), custom_call_target="tpu_custom_call" | custom-call | flops 4294967296 | bytes 16777216 | tf_op jit(solution)/shard_map/dft_piece/pallas_call | solution.py:124
  10.7 7.4 %all-to-all-start = ((bf16[32,256,128]{2,1,0:T(8,128)(2,1)}), bf16[32,256,128]{2,1,0:T(8,128)(2,1)}, u32[]{:S(2)}, u32[]{:S(2)}) async-start(bf16[32,256,128]{2,1,0:T(8,128)(2,1)} %bitcast.16), calls=%async_computation | async-start | bytes 4194304 | tf_op jit(solution)/shard_map/all_to_all | solution.py:331
  18.2 33.6 %dft_piece.7 = bf16[1280,32,128]{2,1,0:T(8,128)(2,1)} custom-call(bf16[1280,2048]{1,0:T(8,128)(2,1)} %constant.27.clone.table_ref, bf16[4,8,128,2048]{3,2,1,0:T(8,128)(2,1)} %pressure_ref.7), custom_call_target="tpu_custom_call" | custom-call | flops 21474836480 | bytes 16777216 | tf_op jit(solution)/shard_map/dft_piece/pallas_call | solution.py:124
  51.8 16.5 %all-to-all-done = bf16[32,256,128]{2,1,0:T(8,128)(2,1)} async-done(((bf16[32,256,128]{2,1,0:T(8,128)(2,1)}), bf16[32,256,128]{2,1,0:T(8,128)(2,1)}, u32[]{:S(2)}, u32[]{:S(2)}) %all-to-all-start) | async-done | bytes 2097184 | tf_op jit(solution)/shard_map/all_to_all | solution.py:331
  68.3 3.9 all-to-all-start.1
  72.2 15.4 %copy.13.refs_2_ = bf16[16,1025,512]{2,1,0:T(8,128)(2,1)} copy(bf16[16,1025,512]{2,0,1:T(8,128)(2,1)} %param.10) | data formatting | bytes 33587200 | tf_op args[1]
  87.5 10.5 %dft_piece.6 = bf16[128,32,128]{2,1,0:T(8,128)(2,1)} custom-call(bf16[128,2048]{1,0:T(8,128)(2,1)} %constant.29.clone.table_ref, bf16[4,8,128,2048]{3,2,1,0:T(8,128)(2,1)} %pressure_ref.7), custom_call_target="tpu_custom_call" | custom-call | flops 2147483648 | bytes 16777216 | tf_op jit(solution)/shard_map/dft_piece/pallas_call | solution.py:124
  98.1 13.2 %dft_piece.4 = bf16[384,32,128]{2,1,0:T(8,128)(2,1)} custom-call(bf16[384,2048]{1,0:T(8,128)(2,1)} %constant.28.clone.table_ref, bf16[4,8,128,2048]{3,2,1,0:T(8,128)(2,1)} %pressure_ref.7), custom_call_target="tpu_custom_call" | custom-call | flops 6442450944 | bytes 16777216 | tf_op jit(solution)/shard_map/dft_piece/pallas_call | solution.py:124
  111.2 17.3 %shells_piece.4.refs_6_ = bf16[16,8200,128]{2,1,0:T(8,128)(2,1)} custom-call(s32[1]{0:T(128)} %bitcast.refs_0_, bf16[32,2,2,2,32,128]{5,4,3,2,1,0:T(8,128)(2,1)} %bitcast.2.refs_1_, bf16[16,1025,512]{2,1,0:T(8,128)(2,1)} %copy.13.refs_2_, bf16[32768,128]{1,0:T(8,128)(2,1)} %bitcast.11, bf16[8,256,256]{2,1,0:T(8,128)(2,1)} %constant.24.clone.refs_4_, ...), custom_call_target="tpu_custom_call" | custom-call | flops 8000000000 | bytes 10000000 | tf_op jit(solution)/shard_map/shells_piece/pallas_call | solution.py:274
  128.6 173.3 %all-to-all-done.1 = bf16[32,1280,128]{2,1,0:T(8,128)(2,1)} async-done(((bf16[32,1280,128]{2,1,0:T(8,128)(2,1)}), bf16[32,1280,128]{2,1,0:T(8,128)(2,1)}, u32[]{:S(2)}, u32[]{:S(2)}) %all-to-all-start.1) | async-done | bytes 10485792 | tf_op jit(solution)/shard_map/all_to_all | solution.py:331
  301.8 3.8 all-to-all-start.3
  305.6 66.1 %shells_piece.5.refs_6_ = bf16[16,8200,128]{2,1,0:T(8,128)(2,1)} custom-call(s32[1]{0:T(128)} %bitcast.refs_0_, bf16[32,2,2,10,32,128]{5,4,3,2,1,0:T(8,128)(2,1)} %bitcast.5.refs_1_, bf16[16,1025,512]{2,1,0:T(8,128)(2,1)} %copy.13.refs_2_, bf16[32768,128]{1,0:T(8,128)(2,1)} %bitcast.12, ...), custom_call_target="tpu_custom_call", output_to_operand_aliasing={{}: (6, {})} | custom-call | flops 40000000000 | bytes 50000000 | tf_op jit(solution)/shard_map/shells_piece/pallas_call | solution.py:274
  371.7 6.3 %all-to-all-done.3 = bf16[32,384,128]{2,1,0:T(8,128)(2,1)} async-done(((bf16[32,384,128]{2,1,0:T(8,128)(2,1)}), bf16[32,384,128]{2,1,0:T(8,128)(2,1)}, u32[]{:S(2)}, u32[]{:S(2)}) %all-to-all-start.3) | async-done | bytes 3145760 | tf_op jit(solution)/shard_map/all_to_all | solution.py:331
  378.0 3.4 all-to-all-start.2
  381.4 23.5 %shells_piece.6.refs_6_ = bf16[16,8200,128]{2,1,0:T(8,128)(2,1)} custom-call(s32[1]{0:T(128)} %bitcast.refs_0_, bf16[32,2,2,3,32,128]{5,4,3,2,1,0:T(8,128)(2,1)} %bitcast.9.refs_1_, bf16[16,1025,512]{2,1,0:T(8,128)(2,1)} %copy.13.refs_2_, bf16[32768,128]{1,0:T(8,128)(2,1)} %bitcast.13, ...), custom_call_target="tpu_custom_call", output_to_operand_aliasing={{}: (6, {})} | custom-call | flops 12000000000 | bytes 15000000 | tf_op jit(solution)/shard_map/shells_piece/pallas_call | solution.py:274
  404.9 4.1 all-to-all-done.2
  409.0 11.1 %shells_piece.7 = bf16[16,8200,128]{2,1,0:T(8,128)(2,1)} custom-call(s32[1]{0:T(128)} %bitcast.refs_0_, bf16[32,2,2,1,32,128]{5,4,3,2,1,0:T(8,128)(2,1)} %bitcast.7.refs_1_, bf16[16,1025,512]{2,1,0:T(8,128)(2,1)} %copy.13.refs_2_, bf16[32768,128]{1,0:T(8,128)(2,1)} %bitcast.14, ...), custom_call_target="tpu_custom_call", output_to_operand_aliasing={{}: (6, {})} | custom-call | flops 4000000000 | bytes 5000000 | tf_op jit(solution)/shard_map/shells_piece/pallas_call | solution.py:274
Async XLA Ops:
  10.7 57.5 %all-to-all-start = ((bf16[32,256,128]{2,1,0:T(8,128)(2,1)}), bf16[32,256,128]{2,1,0:T(8,128)(2,1)}, u32[]{:S(2)}, u32[]{:S(2)}) async-start(bf16[32,256,128]{2,1,0:T(8,128)(2,1)} %bitcast.16), calls=%async_computation | async-start | bytes 4194304 | tf_op jit(solution)/shard_map/all_to_all | solution.py:331
  68.3 233.6 %all-to-all-start.1 = ((bf16[32,1280,128]{2,1,0:T(8,128)(2,1)}), bf16[32,1280,128]{2,1,0:T(8,128)(2,1)}, u32[]{:S(2)}, u32[]{:S(2)}) async-start(bf16[32,1280,128]{2,1,0:T(8,128)(2,1)} %bitcast.15), calls=%async_computation.1 | async-start | bytes 20971520 | tf_op jit(solution)/shard_map/all_to_all | solution.py:331
  301.8 76.2 %all-to-all-start.3 = ((bf16[32,384,128]{2,1,0:T(8,128)(2,1)}), bf16[32,384,128]{2,1,0:T(8,128)(2,1)}, u32[]{:S(2)}, u32[]{:S(2)}) async-start(bf16[32,384,128]{2,1,0:T(8,128)(2,1)} %bitcast.18), calls=%async_computation.3 | async-start | bytes 6291456 | tf_op jit(solution)/shard_map/all_to_all | solution.py:331
  378.0 30.9 %all-to-all-start.2 = ((bf16[32,128,128]{2,1,0:T(8,128)(2,1)}), bf16[32,128,128]{2,1,0:T(8,128)(2,1)}, u32[]{:S(2)}, u32[]{:S(2)}) async-start(bf16[32,128,128]{2,1,0:T(8,128)(2,1)} %bitcast.17), calls=%async_computation.2 | async-start | bytes 2097152 | tf_op jit(solution)/shard_map/all_to_all | solution.py:331

commit v4 on v3

--- a/solution.py
+++ b/solution.py
@@ -10,7 +10,7 @@
 
 LDEG = 1024
 CHUNKS = (2, 10, 3, 1)
-TILE = 512
+TILE = 1024
 VMEM_LIMIT = 63 * 1024 * 1024
 
 
@@ -247,7 +247,7 @@
     rows = jnp.concatenate([leg_ref[0, start:LDEG, :], last], axis=0)
     slabs = [slab_of(start, block) for block in range(TILE // 16)]
     slabs.append(lambda: jnp.tile(factors_at(LDEG - 1), (8, 2)))
-    columns(start, rows, slabs, False)
+    columns(start, rows, slabs, start == 0)
 
 
 def shells_piece(base, received, legendre, radial, pick, turn, output, first, count):

time: 421 us -> 419 us (level)
  Pallas kernels: 186 us -> 181 us
    pallas_call x4, Pallas kernels: 118 us -> 113 us  [shells_piece(): pl.pallas_call(kernel, grid=(count,), in_specs=in_specs, out_specs=pl.Blo...]
  transfers between devices with their start and end apart: 4 -> 4, of which waited for: 4 -> 4; matrix products, arithmetic and copies ran while one was open for 4% -> 4% of each run, Pallas kernels for 39% -> 38%
where the time goes in v4:
time: 419 us
  waiting for transfers between devices  204 us (49%)
  Pallas kernels  181 us (43%)
  starting transfers between devices  18.4 us (4%)
  local copies, waits for them, and re-layouts  15.4 us (4%)
    all_to_all x4, waiting for transfers between devices, on_device(): lax.all_to_all(spread, ('af', 'sa'), split_axis=0, concat_axis=0, tiled=T...  204 us
    pallas_call x4, Pallas kernels, shells_piece(): pl.pallas_call(kernel, grid=(count,), in_specs=in_specs, out_specs=pl.Blo...  113 us
    pallas_call x4, Pallas kernels, dft(): pl.pallas_call(dft_kernel, grid=(4,), in_specs=[pl.BlockSpec((rows, lon_c...  68 us
    all_to_all x4, starting transfers between devices, on_device(): lax.all_to_all(spread, ('af', 'sa'), split_axis=0, concat_axis=0, tiled=T...  18.4 us
    unnamed x1, local copies, waits for them, and re-layouts  15.4 us
  transfers between devices with their start and end apart: 4, of which 4 were waited for; matrix products, arithmetic and copies ran while one was open for 4% of the time, Pallas kernels for 38%

profile of v4, /device:TPU:0, one launch (start us, length us, event | category | flops | bytes accessed | tf_op | source)
XLA Modules:
  0.0 418.7 jit_solution(11132216039809783073)
XLA Ops:
  0.0 10.7 %dft_piece.5 = bf16[256,32,128]{2,1,0:T(8,128)(2,1)} custom-call(bf16[256,2048]{1,0:T(8,128)(2,1)} %constant.26.clone.table_ref, bf16[4,8,128,2048]{3,2,1,0:T(8,128)(2,1)} %pressure_ref.7), custom_call_target="tpu_custom_call" | custom-call | flops 4294967296 | bytes 16777216 | tf_op jit(solution)/shard_map/dft_piece/pallas_call | solution.py:124
  10.7 7.4 %all-to-all-start = ((bf16[32,256,128]{2,1,0:T(8,128)(2,1)}), bf16[32,256,128]{2,1,0:T(8,128)(2,1)}, u32[]{:S(2)}, u32[]{:S(2)}) async-start(bf16[32,256,128]{2,1,0:T(8,128)(2,1)} %bitcast.16), calls=%async_computation | async-start | bytes 4194304 | tf_op jit(solution)/shard_map/all_to_all | solution.py:331
  18.2 33.6 %dft_piece.7 = bf16[1280,32,128]{2,1,0:T(8,128)(2,1)} custom-call(bf16[1280,2048]{1,0:T(8,128)(2,1)} %constant.27.clone.table_ref, bf16[4,8,128,2048]{3,2,1,0:T(8,128)(2,1)} %pressure_ref.7), custom_call_target="tpu_custom_call" | custom-call | flops 21474836480 | bytes 16777216 | tf_op jit(solution)/shard_map/dft_piece/pallas_call | solution.py:124
  51.8 16.5 %all-to-all-done = bf16[32,256,128]{2,1,0:T(8,128)(2,1)} async-done(((bf16[32,256,128]{2,1,0:T(8,128)(2,1)}), bf16[32,256,128]{2,1,0:T(8,128)(2,1)}, u32[]{:S(2)}, u32[]{:S(2)}) %all-to-all-start) | async-done | bytes 2097184 | tf_op jit(solution)/shard_map/all_to_all | solution.py:331
  68.3 3.9 all-to-all-start.1
  72.2 15.4 %copy.13.refs_2_ = bf16[16,1025,512]{2,1,0:T(8,128)(2,1)} copy(bf16[16,1025,512]{2,0,1:T(8,128)(2,1)} %param.10) | data formatting | bytes 33587200 | tf_op args[1]
  87.5 10.5 %dft_piece.6 = bf16[128,32,128]{2,1,0:T(8,128)(2,1)} custom-call(bf16[128,2048]{1,0:T(8,128)(2,1)} %constant.29.clone.table_ref, bf16[4,8,128,2048]{3,2,1,0:T(8,128)(2,1)} %pressure_ref.7), custom_call_target="tpu_custom_call" | custom-call | flops 2147483648 | bytes 16777216 | tf_op jit(solution)/shard_map/dft_piece/pallas_call | solution.py:124
  98.1 13.2 %dft_piece.4 = bf16[384,32,128]{2,1,0:T(8,128)(2,1)} custom-call(bf16[384,2048]{1,0:T(8,128)(2,1)} %constant.28.clone.table_ref, bf16[4,8,128,2048]{3,2,1,0:T(8,128)(2,1)} %pressure_ref.7), custom_call_target="tpu_custom_call" | custom-call | flops 6442450944 | bytes 16777216 | tf_op jit(solution)/shard_map/dft_piece/pallas_call | solution.py:124
  111.2 15.8 %shells_piece.4.refs_6_ = bf16[16,8200,128]{2,1,0:T(8,128)(2,1)} custom-call(s32[1]{0:T(128)} %bitcast.refs_0_, bf16[32,2,2,2,32,128]{5,4,3,2,1,0:T(8,128)(2,1)} %bitcast.2.refs_1_, bf16[16,1025,512]{2,1,0:T(8,128)(2,1)} %copy.13.refs_2_, bf16[32768,128]{1,0:T(8,128)(2,1)} %bitcast.11, bf16[8,256,256]{2,1,0:T(8,128)(2,1)} %constant.24.clone.refs_4_, ...), custom_call_target="tpu_custom_call" | custom-call | flops 8000000000 | bytes 10000000 | tf_op jit(solution)/shard_map/shells_piece/pallas_call | solution.py:274
  127.1 174.8 %all-to-all-done.1 = bf16[32,1280,128]{2,1,0:T(8,128)(2,1)} async-done(((bf16[32,1280,128]{2,1,0:T(8,128)(2,1)}), bf16[32,1280,128]{2,1,0:T(8,128)(2,1)}, u32[]{:S(2)}, u32[]{:S(2)}) %all-to-all-start.1) | async-done | bytes 10485792 | tf_op jit(solution)/shard_map/all_to_all | solution.py:331
  301.8 3.8 all-to-all-start.3
  305.6 65.1 %shells_piece.5.refs_6_ = bf16[16,8200,128]{2,1,0:T(8,128)(2,1)} custom-call(s32[1]{0:T(128)} %bitcast.refs_0_, bf16[32,2,2,10,32,128]{5,4,3,2,1,0:T(8,128)(2,1)} %bitcast.5.refs_1_, bf16[16,1025,512]{2,1,0:T(8,128)(2,1)} %copy.13.refs_2_, bf16[32768,128]{1,0:T(8,128)(2,1)} %bitcast.12, ...), custom_call_target="tpu_custom_call", output_to_operand_aliasing={{}: (6, {})} | custom-call | flops 40000000000 | bytes 50000000 | tf_op jit(solution)/shard_map/shells_piece/pallas_call | solution.py:274
  370.7 7.3 %all-to-all-done.3 = bf16[32,384,128]{2,1,0:T(8,128)(2,1)} async-done(((bf16[32,384,128]{2,1,0:T(8,128)(2,1)}), bf16[32,384,128]{2,1,0:T(8,128)(2,1)}, u32[]{:S(2)}, u32[]{:S(2)}) %all-to-all-start.3) | async-done | bytes 3145760 | tf_op jit(solution)/shard_map/all_to_all | solution.py:331
  378.0 3.4 all-to-all-start.2
  381.4 22.0 %shells_piece.6.refs_6_ = bf16[16,8200,128]{2,1,0:T(8,128)(2,1)} custom-call(s32[1]{0:T(128)} %bitcast.refs_0_, bf16[32,2,2,3,32,128]{5,4,3,2,1,0:T(8,128)(2,1)} %bitcast.9.refs_1_, bf16[16,1025,512]{2,1,0:T(8,128)(2,1)} %copy.13.refs_2_, bf16[32768,128]{1,0:T(8,128)(2,1)} %bitcast.13, ...), custom_call_target="tpu_custom_call", output_to_operand_aliasing={{}: (6, {})} | custom-call | flops 12000000000 | bytes 15000000 | tf_op jit(solution)/shard_map/shells_piece/pallas_call | solution.py:274
  403.4 5.5 %all-to-all-done.2 = bf16[32,128,128]{2,1,0:T(8,128)(2,1)} async-done(((bf16[32,128,128]{2,1,0:T(8,128)(2,1)}), bf16[32,128,128]{2,1,0:T(8,128)(2,1)}, u32[]{:S(2)}, u32[]{:S(2)}) %all-to-all-start.2) | async-done | bytes 1048608 | tf_op jit(solution)/shard_map/all_to_all | solution.py:331
  409.0 9.6 %shells_piece.7 = bf16[16,8200,128]{2,1,0:T(8,128)(2,1)} custom-call(s32[1]{0:T(128)} %bitcast.refs_0_, bf16[32,2,2,1,32,128]{5,4,3,2,1,0:T(8,128)(2,1)} %bitcast.7.refs_1_, bf16[16,1025,512]{2,1,0:T(8,128)(2,1)} %copy.13.refs_2_, bf16[32768,128]{1,0:T(8,128)(2,1)} %bitcast.14, ...), custom_call_target="tpu_custom_call", output_to_operand_aliasing={{}: (6, {})} | custom-call | flops 4000000000 | bytes 5000000 | tf_op jit(solution)/shard_map/shells_piece/pallas_call | solution.py:274
Async XLA Ops:
  10.7 57.5 %all-to-all-start = ((bf16[32,256,128]{2,1,0:T(8,128)(2,1)}), bf16[32,256,128]{2,1,0:T(8,128)(2,1)}, u32[]{:S(2)}, u32[]{:S(2)}) async-start(bf16[32,256,128]{2,1,0:T(8,128)(2,1)} %bitcast.16), calls=%async_computation | async-start | bytes 4194304 | tf_op jit(solution)/shard_map/all_to_all | solution.py:331
  68.3 233.6 %all-to-all-start.1 = ((bf16[32,1280,128]{2,1,0:T(8,128)(2,1)}), bf16[32,1280,128]{2,1,0:T(8,128)(2,1)}, u32[]{:S(2)}, u32[]{:S(2)}) async-start(bf16[32,1280,128]{2,1,0:T(8,128)(2,1)} %bitcast.15), calls=%async_computation.1 | async-start | bytes 20971520 | tf_op jit(solution)/shard_map/all_to_all | solution.py:331
  301.8 76.2 %all-to-all-start.3 = ((bf16[32,384,128]{2,1,0:T(8,128)(2,1)}), bf16[32,384,128]{2,1,0:T(8,128)(2,1)}, u32[]{:S(2)}, u32[]{:S(2)}) async-start(bf16[32,384,128]{2,1,0:T(8,128)(2,1)} %bitcast.18), calls=%async_computation.3 | async-start | bytes 6291456 | tf_op jit(solution)/shard_map/all_to_all | solution.py:331
  378.0 30.9 %all-to-all-start.2 = ((bf16[32,128,128]{2,1,0:T(8,128)(2,1)}), bf16[32,128,128]{2,1,0:T(8,128)(2,1)}, u32[]{:S(2)}, u32[]{:S(2)}) async-start(bf16[32,128,128]{2,1,0:T(8,128)(2,1)} %bitcast.17), calls=%async_computation.2 | async-start | bytes 2097152 | tf_op jit(solution)/shard_map/all_to_all | solution.py:331

commit v5 on v4

--- a/solution.py
+++ b/solution.py
@@ -206,15 +206,11 @@
     def columns(start, rows, slabs, first_tile):
         count = rows.shape[0]
 
-        @pl.when(start < bound)
-        def _():
-            _, harm = legendre_rows(rows, start, 0)
-            harm_ref[0:count] = harm
-
-        @pl.when(start + count > bound)
-        def _():
-            q, harm = legendre_rows(rows, start, 1)
-            harm_ref[0:count] = jnp.where(q >= bound, harm, harm_ref[0:count])
+        half = LDEG // 2
+        _, near = legendre_rows(rows, start, 0)
+        q, far = legendre_rows(rows[half:], start + half, 1)
+        harm_ref[0:half] = near[:half]
+        harm_ref[half:count] = jnp.where(q >= bound, far, near[half:])
 
         fill_copies(harm_ref[0:count])
         if first_tile:

time: 419 us -> 419 us (level)
  Pallas kernels: 181 us -> 170 us
  waiting for transfers between devices: 204 us -> 215 us
    pallas_call x4, Pallas kernels: 113 us -> 102 us  [shells_piece(): pl.pallas_call(kernel, grid=(count,), in_specs=in_specs, out_specs=pl.Blo...]
    all_to_all x4, waiting for transfers between devices: 204 us -> 215 us  [on_device(): lax.all_to_all(spread, ('af', 'sa'), split_axis=0, concat_axis=0, tiled=T...]
  transfers between devices with their start and end apart: 4 -> 4, of which waited for: 4 -> 4; matrix products, arithmetic and copies ran while one was open for 4% -> 4% of each run, Pallas kernels for 38% -> 36%
where the time goes in v5:
time: 419 us
  waiting for transfers between devices  215 us (51%)
  Pallas kernels  170 us (41%)
  starting transfers between devices  18.4 us (4%)
  local copies, waits for them, and re-layouts  15.4 us (4%)
    all_to_all x4, waiting for transfers between devices, on_device(): lax.all_to_all(spread, ('af', 'sa'), split_axis=0, concat_axis=0, tiled=T...  215 us
    pallas_call x4, Pallas kernels, shells_piece(): pl.pallas_call(kernel, grid=(count,), in_specs=in_specs, out_specs=pl.Blo...  102 us
    pallas_call x4, Pallas kernels, dft(): pl.pallas_call(dft_kernel, grid=(4,), in_specs=[pl.BlockSpec((rows, lon_c...  68 us
    all_to_all x4, starting transfers between devices, on_device(): lax.all_to_all(spread, ('af', 'sa'), split_axis=0, concat_axis=0, tiled=T...  18.4 us
    unnamed x1, local copies, waits for them, and re-layouts  15.4 us
  transfers between devices with their start and end apart: 4, of which 4 were waited for; matrix products, arithmetic and copies ran while one was open for 4% of the time, Pallas kernels for 36%

profile of v5, /device:TPU:0, one launch (start us, length us, event | category | flops | bytes accessed | tf_op | source)
XLA Modules:
  0.0 418.6 jit_solution(12651926363702169079)
XLA Ops:
  0.0 10.7 %dft_piece.5 = bf16[256,32,128]{2,1,0:T(8,128)(2,1)} custom-call(bf16[256,2048]{1,0:T(8,128)(2,1)} %constant.26.clone.table_ref, bf16[4,8,128,2048]{3,2,1,0:T(8,128)(2,1)} %pressure_ref.7), custom_call_target="tpu_custom_call" | custom-call | flops 4294967296 | bytes 16777216 | tf_op jit(solution)/shard_map/dft_piece/pallas_call | solution.py:124
  10.7 7.4 %all-to-all-start = ((bf16[32,256,128]{2,1,0:T(8,128)(2,1)}), bf16[32,256,128]{2,1,0:T(8,128)(2,1)}, u32[]{:S(2)}, u32[]{:S(2)}) async-start(bf16[32,256,128]{2,1,0:T(8,128)(2,1)} %bitcast.16), calls=%async_computation | async-start | bytes 4194304 | tf_op jit(solution)/shard_map/all_to_all | solution.py:327
  18.2 33.6 %dft_piece.7 = bf16[1280,32,128]{2,1,0:T(8,128)(2,1)} custom-call(bf16[1280,2048]{1,0:T(8,128)(2,1)} %constant.27.clone.table_ref, bf16[4,8,128,2048]{3,2,1,0:T(8,128)(2,1)} %pressure_ref.7), custom_call_target="tpu_custom_call" | custom-call | flops 21474836480 | bytes 16777216 | tf_op jit(solution)/shard_map/dft_piece/pallas_call | solution.py:124
  51.8 16.5 %all-to-all-done = bf16[32,256,128]{2,1,0:T(8,128)(2,1)} async-done(((bf16[32,256,128]{2,1,0:T(8,128)(2,1)}), bf16[32,256,128]{2,1,0:T(8,128)(2,1)}, u32[]{:S(2)}, u32[]{:S(2)}) %all-to-all-start) | async-done | bytes 2097184 | tf_op jit(solution)/shard_map/all_to_all | solution.py:327
  68.3 3.9 all-to-all-start.1
  72.2 15.4 %copy.13.refs_2_ = bf16[16,1025,512]{2,1,0:T(8,128)(2,1)} copy(bf16[16,1025,512]{2,0,1:T(8,128)(2,1)} %param.10) | data formatting | bytes 33587200 | tf_op args[1]
  87.5 10.5 %dft_piece.6 = bf16[128,32,128]{2,1,0:T(8,128)(2,1)} custom-call(bf16[128,2048]{1,0:T(8,128)(2,1)} %constant.29.clone.table_ref, bf16[4,8,128,2048]{3,2,1,0:T(8,128)(2,1)} %pressure_ref.7), custom_call_target="tpu_custom_call" | custom-call | flops 2147483648 | bytes 16777216 | tf_op jit(solution)/shard_map/dft_piece/pallas_call | solution.py:124
  98.1 13.2 %dft_piece.4 = bf16[384,32,128]{2,1,0:T(8,128)(2,1)} custom-call(bf16[384,2048]{1,0:T(8,128)(2,1)} %constant.28.clone.table_ref, bf16[4,8,128,2048]{3,2,1,0:T(8,128)(2,1)} %pressure_ref.7), custom_call_target="tpu_custom_call" | custom-call | flops 6442450944 | bytes 16777216 | tf_op jit(solution)/shard_map/dft_piece/pallas_call | solution.py:124
  111.2 15.0 %shells_piece.4.refs_6_ = bf16[16,8200,128]{2,1,0:T(8,128)(2,1)} custom-call(s32[1]{0:T(128)} %bitcast.refs_0_, bf16[32,2,2,2,32,128]{5,4,3,2,1,0:T(8,128)(2,1)} %bitcast.2.refs_1_, bf16[16,1025,512]{2,1,0:T(8,128)(2,1)} %copy.13.refs_2_, bf16[32768,128]{1,0:T(8,128)(2,1)} %bitcast.11, bf16[8,256,256]{2,1,0:T(8,128)(2,1)} %constant.24.clone.refs_4_, ...), custom_call_target="tpu_custom_call" | custom-call | flops 8000000000 | bytes 10000000 | tf_op jit(solution)/shard_map/shells_piece/pallas_call | solution.py:270
  126.2 175.6 %all-to-all-done.1 = bf16[32,1280,128]{2,1,0:T(8,128)(2,1)} async-done(((bf16[32,1280,128]{2,1,0:T(8,128)(2,1)}), bf16[32,1280,128]{2,1,0:T(8,128)(2,1)}, u32[]{:S(2)}, u32[]{:S(2)}) %all-to-all-start.1) | async-done | bytes 10485792 | tf_op jit(solution)/shard_map/all_to_all | solution.py:327
  301.8 3.5 all-to-all-start.3
  305.4 57.1 %shells_piece.5.refs_6_ = bf16[16,8200,128]{2,1,0:T(8,128)(2,1)} custom-call(s32[1]{0:T(128)} %bitcast.refs_0_, bf16[32,2,2,10,32,128]{5,4,3,2,1,0:T(8,128)(2,1)} %bitcast.5.refs_1_, bf16[16,1025,512]{2,1,0:T(8,128)(2,1)} %copy.13.refs_2_, bf16[32768,128]{1,0:T(8,128)(2,1)} %bitcast.12, ...), custom_call_target="tpu_custom_call", output_to_operand_aliasing={{}: (6, {})} | custom-call | flops 40000000000 | bytes 50000000 | tf_op jit(solution)/shard_map/shells_piece/pallas_call | solution.py:270
  362.5 15.5 %all-to-all-done.3 = bf16[32,384,128]{2,1,0:T(8,128)(2,1)} async-done(((bf16[32,384,128]{2,1,0:T(8,128)(2,1)}), bf16[32,384,128]{2,1,0:T(8,128)(2,1)}, u32[]{:S(2)}, u32[]{:S(2)}) %all-to-all-start.3) | async-done | bytes 3145760 | tf_op jit(solution)/shard_map/all_to_all | solution.py:327
  378.0 3.6 all-to-all-start.2
  381.6 20.2 %shells_piece.6.refs_6_ = bf16[16,8200,128]{2,1,0:T(8,128)(2,1)} custom-call(s32[1]{0:T(128)} %bitcast.refs_0_, bf16[32,2,2,3,32,128]{5,4,3,2,1,0:T(8,128)(2,1)} %bitcast.9.refs_1_, bf16[16,1025,512]{2,1,0:T(8,128)(2,1)} %copy.13.refs_2_, bf16[32768,128]{1,0:T(8,128)(2,1)} %bitcast.13, ...), custom_call_target="tpu_custom_call", output_to_operand_aliasing={{}: (6, {})} | custom-call | flops 12000000000 | bytes 15000000 | tf_op jit(solution)/shard_map/shells_piece/pallas_call | solution.py:270
  401.8 7.1 %all-to-all-done.2 = bf16[32,128,128]{2,1,0:T(8,128)(2,1)} async-done(((bf16[32,128,128]{2,1,0:T(8,128)(2,1)}), bf16[32,128,128]{2,1,0:T(8,128)(2,1)}, u32[]{:S(2)}, u32[]{:S(2)}) %all-to-all-start.2) | async-done | bytes 1048608 | tf_op jit(solution)/shard_map/all_to_all | solution.py:327
  409.0 9.5 %shells_piece.7 = bf16[16,8200,128]{2,1,0:T(8,128)(2,1)} custom-call(s32[1]{0:T(128)} %bitcast.refs_0_, bf16[32,2,2,1,32,128]{5,4,3,2,1,0:T(8,128)(2,1)} %bitcast.7.refs_1_, bf16[16,1025,512]{2,1,0:T(8,128)(2,1)} %copy.13.refs_2_, bf16[32768,128]{1,0:T(8,128)(2,1)} %bitcast.14, ...), custom_call_target="tpu_custom_call", output_to_operand_aliasing={{}: (6, {})} | custom-call | flops 4000000000 | bytes 5000000 | tf_op jit(solution)/shard_map/shells_piece/pallas_call | solution.py:270
Async XLA Ops:
  10.7 57.5 %all-to-all-start = ((bf16[32,256,128]{2,1,0:T(8,128)(2,1)}), bf16[32,256,128]{2,1,0:T(8,128)(2,1)}, u32[]{:S(2)}, u32[]{:S(2)}) async-start(bf16[32,256,128]{2,1,0:T(8,128)(2,1)} %bitcast.16), calls=%async_computation | async-start | bytes 4194304 | tf_op jit(solution)/shard_map/all_to_all | solution.py:327
  68.3 233.6 %all-to-all-start.1 = ((bf16[32,1280,128]{2,1,0:T(8,128)(2,1)}), bf16[32,1280,128]{2,1,0:T(8,128)(2,1)}, u32[]{:S(2)}, u32[]{:S(2)}) async-start(bf16[32,1280,128]{2,1,0:T(8,128)(2,1)} %bitcast.15), calls=%async_computation.1 | async-start | bytes 20971520 | tf_op jit(solution)/shard_map/all_to_all | solution.py:327
  301.8 76.2 %all-to-all-start.3 = ((bf16[32,384,128]{2,1,0:T(8,128)(2,1)}), bf16[32,384,128]{2,1,0:T(8,128)(2,1)}, u32[]{:S(2)}, u32[]{:S(2)}) async-start(bf16[32,384,128]{2,1,0:T(8,128)(2,1)} %bitcast.18), calls=%async_computation.3 | async-start | bytes 6291456 | tf_op jit(solution)/shard_map/all_to_all | solution.py:327
  378.0 30.9 %all-to-all-start.2 = ((bf16[32,128,128]{2,1,0:T(8,128)(2,1)}), bf16[32,128,128]{2,1,0:T(8,128)(2,1)}, u32[]{:S(2)}, u32[]{:S(2)}) async-start(bf16[32,128,128]{2,1,0:T(8,128)(2,1)} %bitcast.17), calls=%async_computation.2 | async-start | bytes 2097152 | tf_op jit(solution)/shard_map/all_to_all | solution.py:327
